TPU v7x, 32 devices: a whole 2x2x4 slice. The times are simulated.
32 devices in a mesh: section: 2 (over x), ctx: 8 (over z, y), wsh: 2 (over core).
Axes of the slice: x: 2, y: 2, z: 4, core: 2. Of those that a mesh axis runs over, the one named last changes fastest.
Arguments:
- inputs: bfloat16 [2, 2, 1024, 1024], P(None, 'wsh', 'ctx'), may hold values from -6 to 6
- cotangent: bfloat16 [2, 2, 1024, 1024], P(None, 'wsh', 'ctx'), may hold values from -6 to 6
- block_pair: int32 [8], replicated, may hold values from 0 to 7, each once
- qkv_weight: bfloat16 [2, 1024, 3072], P('section', 'wsh'), may hold values from -0.1875 to 0.1875
- qkv_bias: bfloat16 [2, 3072], P('section', 'wsh'), may hold values from -1.75 to 1.75
- proj_weight: bfloat16 [2, 1024, 1024], P('section', 'wsh'), may hold values from -3 to 3
- proj_bias: bfloat16 [2, 1024], P('section', 'wsh'), may hold values from -1.75 to 1.75
- up_weight: bfloat16 [2, 1024, 4096], P('section', 'wsh'), may hold values from -0.1875 to 0.1875
- up_bias: bfloat16 [2, 4096], P('section', 'wsh'), may hold values from -1.75 to 1.75
- down_weight: bfloat16 [2, 4096, 1024], P('section', 'wsh'), may hold values from -0.09375 to 0.09375
- down_bias: bfloat16 [2, 1024], P('section', 'wsh'), may hold values from -1.75 to 1.75
- attn_gain: bfloat16 [2, 1024], P('section', 'wsh'), may hold values from 0.099609375 to 1.8984375
- attn_shift: bfloat16 [2, 1024], P('section', 'wsh'), may hold values from -1.75 to 1.75
- mlp_gain: bfloat16 [2, 1024], P('section', 'wsh'), may hold values from 0.099609375 to 1.8984375
- mlp_shift: bfloat16 [2, 1024], P('section', 'wsh'), may hold values from -1.75 to 1.75
Outputs:
- layer_out: bfloat16 [2, 2, 2, 1024, 1024], P('section', None, 'wsh', 'ctx')
- input_grad: bfloat16 [2, 2, 2, 1024, 1024], P('section', None, 'wsh', 'ctx')
- grad_qkv_weight: float32 [2, 1024, 3072], P('section', 'wsh')
- grad_qkv_bias: float32 [2, 3072], P('section', 'wsh')
- grad_proj_weight: float32 [2, 1024, 1024], P('section', 'wsh')
- grad_proj_bias: float32 [2, 1024], P('section', 'wsh')
- grad_up_weight: float32 [2, 1024, 4096], P('section', 'wsh')
- grad_up_bias: float32 [2, 4096], P('section', 'wsh')
- grad_down_weight: float32 [2, 4096, 1024], P('section', 'wsh')
- grad_down_bias: float32 [2, 1024], P('section', 'wsh')
- grad_attn_gain: float32 [2, 1024], P('section', 'wsh')
- grad_attn_shift: float32 [2, 1024], P('section', 'wsh')
- grad_mlp_gain: float32 [2, 1024], P('section', 'wsh')
- grad_mlp_shift: float32 [2, 1024], P('section', 'wsh')
Inputs may be any that keep to these rules, and one draw needn't show every extreme that they name: The index d of ctx stores for every sequence the causal blocks block_pair[d] and 15 - block_pair[d], in that order; each value occurs once.
All inputs are finite; a program needn't handle non-finite values.
Results may differ from a plain program's by a relative error of at most 0.015.
Values may be sent and summed in bfloat16 or wider, within the bound.
No kernel may reach another device: no remote copies, remote signals or barrier semaphores. Data moves between devices by JAX's collectives and lax.ppermute only.
A program may use at most 320 MiB of HBM per device.

v0:
```python
import functools

import jax
import jax.numpy as jnp
from jax import lax
from jax.experimental import pallas as pl
from jax.experimental.pallas import tpu as pltpu
from jax.sharding import PartitionSpec as P

HEADS = 16
ROT = 16
NORM_EPS = 1e-05
ROPE_BASE = 10000.0
MASKED_SCORE = -1e30
LANES = 128
VMEM_LIMIT = 56 * 1024 * 1024
TAIL_LIMIT = 56 * 1024 * 1024
RING_LIMIT = 50 * 1024 * 1024
INV_SQRT2 = 0.7071067811865476
INV_SQRT_2PI = 0.3989422804014327

f32 = jnp.float32
bf16 = jnp.bfloat16


def dot_nn(left, right):
    return lax.dot_general(left, right, (((1,), (0,)), ((), ())), preferred_element_type=f32)


def dot_nt(left, right):
    return lax.dot_general(left, right, (((1,), (1,)), ((), ())), preferred_element_type=f32)


def params_of(limit):
    return dict(
        compiler_params=pltpu.CompilerParams(vmem_limit_bytes=limit),
        cost_estimate=pl.CostEstimate(flops=1, bytes_accessed=1, transcendentals=0),
    )


def whole(shape):
    rank = len(shape)
    return pl.BlockSpec(shape, lambda *args: (0,) * rank)


def shape_of(shape, dtype):
    return jax.ShapeDtypeStruct(shape, dtype)


def rope(vals, tab_ref):
    return (
        vals * tab_ref[0]
        + pltpu.roll(vals, LANES - ROT // 2, 1) * tab_ref[1]
        + pltpu.roll(vals, ROT // 2, 1) * tab_ref[2]
    )


def unrope(vals, tab_ref):
    return (
        vals * tab_ref[0]
        - pltpu.roll(vals, LANES - ROT // 2, 1) * tab_ref[1]
        - pltpu.roll(vals, ROT // 2, 1) * tab_ref[2]
    )


def normalized(hidden):
    row_mean = jnp.mean(hidden, axis=-1, keepdims=True)
    centered = hidden - row_mean
    spread = jnp.mean(centered * centered, axis=-1, keepdims=True)
    scale = lax.rsqrt(spread + NORM_EPS)
    return centered * scale, scale


def start_all(copies):
    for copy in copies:
        copy.start()
    return copies


def wait_all(copies):
    for copy in copies:
        copy.wait()


def qkv_kernel(own_given, wsh_ref, inputs, weights, outputs, buf, sems):
    half, dim = buf.shape[2:]
    copies = start_all(
        [
            pltpu.make_async_copy(
                weight.at[:, pl.ds(part * dim, dim)], buf.at[part, side], sems.at[part, side]
            )
            for part in range(3)
            for side, weight in enumerate(weights)
        ]
    )
    out, x_out, own, oth = outputs
    x = inputs[0].ref()[...]
    if not own_given:
        x = jnp.where(wsh_ref[1] == 1, x, inputs[4].ref()[...])
    x_out.ref[...] = x
    x_out.send()
    xhat, _ = normalized(x.astype(f32))
    vec_ref, bias_ref, tab_ref = (item.ref() for item in inputs[1:4])
    na = (xhat * vec_ref[0:1] + vec_ref[1:2]).astype(bf16)
    nm = (xhat * vec_ref[2:3] + vec_ref[3:4]).astype(bf16)
    first = wsh_ref[0] == 0
    for i, rows in enumerate((na, nm)):
        own.ref[i] = jnp.where(first, rows[:, :half], rows[:, half:])
        oth.ref[i] = jnp.where(first, rows[:, half:], rows[:, :half])
    own.send()
    oth.send()
    for part in range(3):
        wait_all(copies[2 * part : 2 * part + 2])
        for at in range(0, dim, 2 * LANES):
            cols = slice(at, at + 2 * LANES)
            res = (
                dot_nn(own.ref[0], buf[part, 0, :, cols])
                + dot_nn(oth.ref[0], buf[part, 1, :, cols])
                + bias_ref[:, part * dim + at : part * dim + at + 2 * LANES]
            )
            for i in range(2):
                vals = res[:, i * LANES : (i + 1) * LANES]
                if part < 2:
                    vals = rope(vals, tab_ref)
                out.ref[at // LANES + i, part] = vals.astype(bf16)


def layer_of(shape, index):
    return pl.BlockSpec((pl.squeezed,) + shape, lambda *args: (index, 0, 0))


HERE = pl.BlockSpec(memory_space=pltpu.VMEM)
SCALARS = pl.BlockSpec(memory_space=pltpu.SMEM)
ANYWHERE = pl.BlockSpec(memory_space=pl.ANY)
IN_HBM = pl.BlockSpec(memory_space=pltpu.HBM)


class Arriving:
    def __init__(self, buf, copy=None):
        self.buf, self.copy = buf, copy

    def ref(self):
        if self.copy is not None:
            self.copy.wait()
            self.copy = None
        return self.buf


class Leaving:
    def __init__(self, buf, copy=None):
        self.ref, self.copy, self.sent = buf, copy, copy is None

    def send(self):
        if not self.sent:
            self.copy.start()
            self.sent = True


def local_kernel(body, near_in, near_out, scalars, weights, followed, *refs):
    refs = list(refs)

    def take(number):
        taken = refs[:number]
        del refs[:number]
        return taken

    scalar_refs, array_refs = take(scalars), take(len(near_in))
    weight_refs, _, out_refs = take(weights), take(followed), take(len(near_out))
    in_sems, out_sems = take(2)
    inputs, outputs = [], []
    for i, (near, ref) in enumerate(zip(near_in, array_refs)):
        if near:
            inputs.append(Arriving(ref))
        else:
            buf = take(1)[0]
            copy = pltpu.make_async_copy(ref, buf, in_sems.at[i])
            copy.start()
            inputs.append(Arriving(buf, copy))
    for i, (near, ref) in enumerate(zip(near_out, out_refs)):
        if near:
            outputs.append(Leaving(ref))
        else:
            buf = take(1)[0]
            outputs.append(Leaving(buf, pltpu.make_async_copy(buf, ref, out_sems.at[i])))
    body(*scalar_refs, inputs, weight_refs, outputs, *refs)
    for item in inputs:
        item.ref()
    for item in outputs:
        item.send()
    for item in outputs:
        if item.copy is not None:
            item.copy.wait()


def far(array):
    return (array,)


def local_call(body, name, scalars, arrays, weights, out_shape, scratch=(), after=(), limit=VMEM_LIMIT):
    near_in = [not isinstance(a, tuple) for a in arrays]
    near_out = [not isinstance(o, tuple) for o in out_shape]
    raw_out = [isinstance(o, list) for o in out_shape]
    arrays = [a if near else a[0] for a, near in zip(arrays, near_in)]
    shapes = [o if near and not raw else o[0] for o, near, raw in zip(out_shape, near_out, raw_out)]
    far_bufs = [
        pltpu.VMEM(a.shape, a.dtype)
        for a, near in zip(arrays + shapes, near_in + near_out)
        if not near
    ]
    return pl.pallas_call(
        functools.partial(
            local_kernel, body, near_in, near_out, len(scalars), len(weights), len(after)
        ),
        in_specs=[SCALARS] * len(scalars)
        + [HERE if near else IN_HBM for near in near_in]
        + [IN_HBM] * len(weights)
        + [ANYWHERE] * len(after),
        out_specs=[HERE if near and not raw else IN_HBM for near, raw in zip(near_out, raw_out)],
        out_shape=shapes,
        scratch_shapes=[
            pltpu.SemaphoreType.DMA((len(arrays) + 1,)),
            pltpu.SemaphoreType.DMA((len(shapes),)),
        ]
        + far_bufs
        + list(scratch),
        name=name,
        **params_of(limit),
    )(*scalars, *arrays, *weights, *after)


def qkv_call(given, got, vecs, qkv_b, tab, w_own, w_oth, wsh):
    rows, dim = given.shape
    half = w_own.shape[0]
    pairs = dim // LANES
    return local_call(
        functools.partial(qkv_kernel, got is None),
        "qkv_proj",
        [wsh],
        [given, vecs, qkv_b, tab] if got is None else [far(given), vecs, qkv_b, tab, got],
        [w_own, w_oth],
        [far(shape_of((pairs, 3, rows, LANES), bf16)), far(shape_of((rows, dim), bf16))]
        + [far(shape_of((2, rows, half), bf16))] * 2,
        [pltpu.VMEM((3, 2, half, dim), bf16), pltpu.SemaphoreType.DMA((3, 2))],
    )


FF_TILE = 1024
FF_PIECE = 512


def ff_tiles(wsh_ref, up_own, up_oth, dn_own, dn_oth, up_buf, dn_buf, sems):
    own = dn_own.shape[0] // FF_TILE
    tiles = []
    for t in range(2 * own):
        start = pl.multiple_of(((wsh_ref[0] * own + t) % (2 * own)) * FF_TILE, FF_TILE)
        cols = pl.ds(start, FF_TILE)
        down = (dn_own if t < own else dn_oth).at[pl.ds((t % own) * FF_TILE, FF_TILE)]
        copies = [
            pltpu.make_async_copy(up_own.at[:, cols], up_buf.at[t, 0], sems.at[t, 0]),
            pltpu.make_async_copy(up_oth.at[:, cols], up_buf.at[t, 1], sems.at[t, 1]),
            pltpu.make_async_copy(down, dn_buf.at[t], sems.at[t, 2]),
        ]
        tiles.append((t, start, start_all(copies)))
    for t, start, copies in tiles:
        wait_all(copies)
        for at in range(0, FF_TILE, FF_PIECE):
            row = (t % own) * FF_TILE + at
            place = pl.ds(pl.multiple_of(start + at, FF_PIECE), FF_PIECE)
            yield t, place, t < own, slice(row, row + FF_PIECE), slice(at, at + FF_PIECE)


def ff_scratch(half, ff, dim):
    tiles = ff // FF_TILE
    return [
        pltpu.VMEM((tiles, 2, half, FF_TILE), bf16),
        pltpu.VMEM((tiles, FF_TILE, dim), bf16),
        pltpu.SemaphoreType.DMA((tiles, 3)),
    ]


def mlp_kernel(save, wsh_ref, inputs, weights, outputs, up_buf, dn_buf, sems):
    out_ref = outputs[0].ref
    started = False
    for t, place, held, rows, piece in ff_tiles(wsh_ref, *weights, up_buf, dn_buf, sems):
        own_ref, oth_ref, up_b, down_b = (item.ref() for item in inputs)
        if not started:
            out_ref[...] = jnp.broadcast_to(down_b[...], out_ref.shape)
            started = True
        pre = (
            dot_nn(own_ref[1], up_buf[t, 0, :, piece])
            + dot_nn(oth_ref[1], up_buf[t, 1, :, piece])
            + up_b[:, place]
        )
        gate = 0.5 + 0.5 * lax.erf(pre * INV_SQRT2)
        act = (pre * gate).astype(bf16)
        if save:
            slope = gate + pre * (INV_SQRT_2PI * jnp.exp(-0.5 * pre * pre))
            outputs[1].ref[place] = slope.astype(bf16).T
            outputs[2 if held else 3].ref[rows] = act.T
            if not held:
                outputs[2].send()
        out_ref[...] += dot_nn(act, dn_buf[t, piece])


def mlp_call(own, oth, up_b, down_b, up_own, up_oth, dn_own, dn_oth, wsh, save):
    rows, half = own.shape[1:]
    dim = dn_own.shape[1]
    ff = up_own.shape[1]
    out_shape = [far(shape_of((rows, dim), f32))]
    if save:
        out_shape += [far(shape_of((ff, rows), bf16))]
        out_shape += [far(shape_of((ff // 2, rows), bf16))] * 2
    return local_call(
        functools.partial(mlp_kernel, save),
        "mlp_forward",
        [wsh],
        [far(own), far(oth), up_b, down_b],
        [up_own, up_oth, dn_own, dn_oth],
        out_shape,
        ff_scratch(half, ff, dim),
    )


def mlp_back_kernel(wsh_ref, inputs, weights, outputs, acc_own, acc_oth, up_buf, dn_buf, sems):
    du, dnm = outputs
    half = acc_own.shape[0]
    acc_own[...] = jnp.zeros(acc_own.shape, f32)
    acc_oth[...] = jnp.zeros(acc_oth.shape, f32)
    for t, place, _, _, piece in ff_tiles(wsh_ref, *weights, up_buf, dn_buf, sems):
        dy_ref, slope_ref = (item.ref() for item in inputs)
        dact = dot_nt(dn_buf[t, piece], dy_ref[...])
        vals = (dact * slope_ref[place].astype(f32)).astype(bf16)
        du.ref[place] = vals
        acc_own[...] += dot_nn(up_buf[t, 0, :, piece], vals)
        acc_oth[...] += dot_nn(up_buf[t, 1, :, piece], vals)
    du.send()
    first = wsh_ref[0] == 0
    dnm.ref[:, :half] = jnp.where(first, acc_own[...], acc_oth[...]).T
    dnm.ref[:, half:] = jnp.where(first, acc_oth[...], acc_own[...]).T


def mlp_back_call(dy, slope, up_own, up_oth, dn_own, dn_oth, wsh, after, limit):
    rows, dim = dy.shape
    half, ff = up_own.shape
    return local_call(
        mlp_back_kernel,
        "mlp_backward",
        [wsh],
        [far(dy), far(slope)],
        [up_own, up_oth, dn_own, dn_oth],
        [far(shape_of(slope.shape, bf16)), far(shape_of((rows, dim), f32))],
        [pltpu.VMEM((half, rows), f32), pltpu.VMEM((half, rows), f32)] + ff_scratch(half, ff, dim),
        after,
        limit,
    )


def sort_in(loc_ref, ref, dst, half_rows, part=None):
    for block in range(dst.shape[0] // half_rows):
        place = loc_ref[block]
        rows = pl.ds(pl.multiple_of((place % 2) * half_rows, half_rows), half_rows)
        if part is None:
            vals = ref[place // 2, rows, :]
        else:
            vals = ref[place // 2, part, rows, :]
        dst[block * half_rows : (block + 1) * half_rows] = vals


def sort_out(loc_ref, vals, ref, half_rows, part=None):
    for block in range(vals.shape[0] // half_rows):
        place = loc_ref[block]
        rows = pl.ds(pl.multiple_of((place % 2) * half_rows, half_rows), half_rows)
        piece = vals[block * half_rows : (block + 1) * half_rows]
        if part is None:
            ref[place // 2, rows, :] = piece
        else:
            ref[place // 2, part, rows, :] = piece


def head_of(vals, head):
    lane = lax.broadcasted_iota(jnp.int32, vals.shape, 1)
    return jnp.where(lane // (LANES // 2) == head, vals, jnp.zeros_like(vals))


def scores_of(keys, queries, scale, diagonal):
    scores = dot_nt(keys, queries) * scale
    if diagonal:
        key_at = lax.broadcasted_iota(jnp.int32, scores.shape, 0)
        query_at = lax.broadcasted_iota(jnp.int32, scores.shape, 1)
        scores = jnp.where(key_at <= query_at, scores, MASKED_SCORE)
    return scores


def attend_kernel(tile, loc_ref, inputs, weights, outputs, q_s, k_s, v_s, vt_s, o_s):
    qkv_ref = inputs[0].ref()
    o_ref, lse_ref = (item.ref for item in outputs)
    half_rows = qkv_ref.shape[2] // 2
    seq = q_s.shape[0]
    head_size = LANES // 2
    scale = head_size**-0.5
    sort_in(loc_ref, qkv_ref, q_s, half_rows, 0)
    sort_in(loc_ref, qkv_ref, k_s, half_rows, 1)
    sort_in(loc_ref, qkv_ref, v_s, half_rows, 2)
    vt_s[...] = v_s[...].T
    for t in range(seq // tile):
        rows = slice(t * tile, (t + 1) * tile)
        queries = q_s[rows]
        outs = []
        for head in range(2):
            picked = head_of(queries, head)
            parts = [
                scores_of(k_s[i * tile : (i + 1) * tile], picked, scale, i == t)
                for i in range(t + 1)
            ]
            top = functools.reduce(
                jnp.maximum, [jnp.max(p, axis=0, keepdims=True) for p in parts]
            )
            parts = [jnp.exp(p - top) for p in parts]
            total = sum(jnp.sum(p, axis=0, keepdims=True) for p in parts)
            lse_ref[head : head + 1, rows] = top + jnp.log(total)
            inverse = 1.0 / total
            acc = None
            for i, p in enumerate(parts):
                term = dot_nn(
                    vt_s[head * head_size : (head + 1) * head_size, i * tile : (i + 1) * tile],
                    (p * inverse).astype(bf16),
                )
                acc = term if acc is None else acc + term
            outs.append(acc)
        o_s[rows] = jnp.concatenate(outs, axis=0).T.astype(bf16)
    sort_out(loc_ref, o_s, o_ref, half_rows)


def attend_call(qkv, loc, after):
    count, _, rows, _ = qkv.shape
    seq = count * rows
    return local_call(
        functools.partial(attend_kernel, 256),
        "attention",
        [loc],
        [qkv],
        [],
        [far(shape_of((count, rows, LANES), bf16)), far(shape_of((2, seq), f32))],
        [
            pltpu.VMEM((seq, LANES), bf16),
            pltpu.VMEM((seq, LANES), bf16),
            pltpu.VMEM((seq, LANES), bf16),
            pltpu.VMEM((LANES, seq), bf16),
            pltpu.VMEM((seq, LANES), bf16),
        ],
        after,
    )


def attend_back_kernel(
    tile, part, loc_ref, inputs, weights, outputs, q_s, k_s, v_s, da_s, kt_s, dq_s, dk_s, dv_s
):
    da_ref, qkv_ref, lse_ref = (item.ref() for item in inputs)
    out_ref = outputs[0].ref
    half_rows = qkv_ref.shape[2] // 2
    seq = q_s.shape[0]
    head_size = LANES // 2
    scale = head_size**-0.5
    sort_in(loc_ref, qkv_ref, q_s, half_rows, 0)
    sort_in(loc_ref, qkv_ref, k_s, half_rows, 1)
    sort_in(loc_ref, qkv_ref, v_s, half_rows, 2)
    sort_in(loc_ref, da_ref, da_s, half_rows, part)
    kt_s[...] = k_s[...].T
    dk_s[...] = jnp.zeros(dk_s.shape, f32)
    dv_s[...] = jnp.zeros(dv_s.shape, f32)
    for t in range(seq // tile):
        rows = slice(t * tile, (t + 1) * tile)
        outs = []
        for head in range(2):
            queries = head_of(q_s[rows], head)
            grads = head_of(da_s[rows], head)
            lse = lse_ref[head : head + 1, rows]
            probs, dprobs, row_dot = [], [], 0.0
            for i in range(t + 1):
                keys = slice(i * tile, (i + 1) * tile)
                p = jnp.exp(scores_of(k_s[keys], queries, scale, i == t) - lse)
                dp = dot_nt(v_s[keys], grads)
                row_dot = row_dot + jnp.sum(p * dp, axis=0, keepdims=True)
                dv_s[keys] += dot_nn(p.astype(bf16), grads)
                probs.append(p)
                dprobs.append(dp)
            acc = None
            for i in range(t + 1):
                keys = slice(i * tile, (i + 1) * tile)
                ds = (probs[i] * (dprobs[i] - row_dot) * scale).astype(bf16)
                dk_s[keys] += dot_nn(ds, queries)
                term = dot_nn(kt_s[head * head_size : (head + 1) * head_size, keys], ds)
                acc = term if acc is None else acc + term
            outs.append(acc)
        dq_s[rows] = jnp.concatenate(outs, axis=0).T.astype(bf16)
    sort_out(loc_ref, dq_s, out_ref, half_rows, 0)
    k_s[...] = dk_s[...].astype(bf16)
    v_s[...] = dv_s[...].astype(bf16)
    sort_out(loc_ref, k_s, out_ref, half_rows, 1)
    sort_out(loc_ref, v_s, out_ref, half_rows, 2)


def attend_back_call(qkv, da, lse, loc, after, limit):
    count, _, rows, _ = qkv.shape
    seq = count * rows
    part = 0 if da.ndim == 4 else None
    (res,) = local_call(
        functools.partial(attend_back_kernel, 256, part),
        "attention_backward",
        [loc],
        [da, far(qkv), far(lse)],
        [],
        [far(shape_of(qkv.shape, bf16))],
        [pltpu.VMEM((seq, LANES), bf16)] * 4
        + [pltpu.VMEM((LANES, seq), bf16), pltpu.VMEM((seq, LANES), bf16)]
        + [pltpu.VMEM((seq, LANES), f32)] * 2,
        after,
        limit,
    )
    return res


def by_head(parts):
    pairs, rows, lanes = parts.shape
    return jnp.transpose(parts, (1, 0, 2)).reshape(rows, HEADS, pairs * lanes // HEADS)


def by_pair(heads):
    rows = heads.shape[0]
    return jnp.transpose(heads.reshape(rows, -1, LANES), (1, 0, 2))


def wide_scores(queries, keys, query_pos, key_pos):
    raw = jnp.einsum("qhd,khd->hqk", queries, keys, preferred_element_type=f32)
    allowed = (query_pos[:, None] >= key_pos[None, :])[None]
    return jnp.where(allowed, raw * queries.shape[-1] ** (-0.5), MASKED_SCORE)


def key_blocks(arrays, rows):
    return tuple(a.reshape((a.shape[0] // rows, rows) + a.shape[1:]) for a in arrays)


def wide_attend(qkv, query_pos, key_pos):
    queries = by_head(qkv[:, 0])
    keys = lax.all_gather(by_head(qkv[:, 1]), "ctx", axis=0, tiled=True)
    values = lax.all_gather(by_head(qkv[:, 2]), "ctx", axis=0, tiled=True)
    block = min(512, keys.shape[0])
    split = key_blocks((keys, values, key_pos), block)
    rows, _, head_size = queries.shape

    def max_step(carry, block_in):
        top, total = carry
        scores = wide_scores(queries, block_in[0], query_pos, block_in[2])
        new_top = jnp.maximum(top, jnp.max(scores, axis=-1))
        part = jnp.sum(jnp.exp(scores - new_top[..., None]), axis=-1)
        return ((new_top, total * jnp.exp(top - new_top) + part), None)

    start = (jnp.full((HEADS, rows), MASKED_SCORE, f32), jnp.zeros((HEADS, rows), f32))
    (top, total), _ = lax.scan(max_step, start, split)
    lse = top + jnp.log(total)

    def value_step(running, block_in):
        scores = wide_scores(queries, block_in[0], query_pos, block_in[2])
        probs = jnp.exp(scores - lse[..., None]).astype(bf16)
        term = jnp.einsum("hqk,khd->qhd", probs, block_in[1], preferred_element_type=f32)
        return (running + term, None)

    attended, _ = lax.scan(value_step, jnp.zeros((rows, HEADS, head_size), f32), split)
    return by_pair(attended.astype(bf16)), (queries, keys, values, lse)


def wide_attend_back(kept, da, query_pos, key_pos):
    queries, keys, values, lse = kept
    grads = by_head(da)
    block = min(512, keys.shape[0])
    split = key_blocks((keys, values, key_pos), block)
    scale = queries.shape[-1] ** (-0.5)

    def pieces(block_in):
        scores = wide_scores(queries, block_in[0], query_pos, block_in[2])
        probs = jnp.exp(scores - lse[..., None])
        dprobs = jnp.einsum("qhd,khd->hqk", grads, block_in[1], preferred_element_type=f32)
        return probs, dprobs

    def dot_step(running, block_in):
        probs, dprobs = pieces(block_in)
        return (running + jnp.sum(probs * dprobs, axis=-1), None)

    row_dot, _ = lax.scan(dot_step, jnp.zeros(lse.shape, f32), split)

    def key_step(running, block_in):
        probs, dprobs = pieces(block_in)
        ds = (scale * probs * (dprobs - row_dot[..., None])).astype(bf16)
        running = running + jnp.einsum("hqk,khd->qhd", ds, block_in[0], preferred_element_type=f32)
        dk = jnp.einsum("hqk,qhd->khd", ds, queries, preferred_element_type=f32)
        dv = jnp.einsum("hqk,qhd->khd", probs.astype(bf16), grads, preferred_element_type=f32)
        return (running, (dk.astype(bf16), dv.astype(bf16)))

    dq, (dk, dv) = lax.scan(key_step, jnp.zeros(queries.shape, f32), split)
    dk, dv = (
        lax.psum_scatter(part.reshape(keys.shape), "ctx", scatter_dimension=0, tiled=True)
        for part in (dk, dv)
    )
    return jnp.stack([by_pair(dq.astype(bf16)), by_pair(dk), by_pair(dv)], axis=1)


def lanes_of(ref):
    return jnp.concatenate([ref[i] for i in range(ref.shape[0])], axis=1)


def both_halves(w_own, w_oth, buf, sems):
    return start_all(
        [
            pltpu.make_async_copy(weight, buf.at[side], sems.at[side])
            for side, weight in enumerate((w_own, w_oth))
        ]
    )


def half_scratch(weight):
    return [pltpu.VMEM((2,) + weight.shape, bf16), pltpu.SemaphoreType.DMA((2,))]


def proj_kernel(part, wsh_ref, inputs, weights, outputs, buf, sems):
    copies = both_halves(*weights, buf, sems)
    y, own, oth = outputs
    half = buf.shape[1]
    first = wsh_ref[0] == 0
    a_ref = inputs[0].ref()
    a = lanes_of(a_ref if part is None else a_ref.at[:, part])
    own.ref[...] = jnp.where(first, a[:, :half], a[:, half:])
    oth.ref[...] = jnp.where(first, a[:, half:], a[:, :half])
    own.send()
    oth.send()
    bias_ref, x_ref, mlp_ref = (item.ref() for item in inputs[1:])
    wait_all(copies)
    attn = dot_nn(own.ref[...], buf[0]) + dot_nn(oth.ref[...], buf[1]) + bias_ref[...]
    y.ref[...] = (x_ref[...].astype(f32) + attn + mlp_ref[...]).astype(bf16)


def proj_call(a, x, mlp, bias, p_own, p_oth, wsh, after, limit):
    rows, dim = x.shape
    half = p_own.shape[0]
    return local_call(
        functools.partial(proj_kernel, 1 if a.ndim == 4 else None),
        "attn_out",
        [wsh],
        [a, bias, far(x), far(mlp)],
        [p_own, p_oth],
        [far(shape_of((rows, dim), bf16))] + [far(shape_of((rows, half), bf16))] * 2,
        half_scratch(p_own),
        after,
        limit,
    )


def da_kernel(own_given, wsh_ref, inputs, weights, outputs, buf, sems):
    copies = both_halves(*weights, buf, sems)
    out_ref, dy_out = outputs[0].ref, outputs[1]
    dy = inputs[0].ref()[...]
    if not own_given:
        dy = jnp.where(wsh_ref[1] == 1, inputs[1].ref()[...], dy)
    dy_out.ref[...] = dy
    dy_out.send()
    wsh = wsh_ref[0]
    joined = len(out_ref.shape) == 4
    if joined:
        out_ref[:, 1] = inputs[2].ref()[...]
    count = out_ref.shape[0] // 2
    for place, side in ((wsh * count, 0), ((1 - wsh) * count, 1)):
        copies[side].wait()
        part = dot_nt(dy, buf[side]).astype(bf16)
        for i in range(count):
            vals = part[:, i * LANES : (i + 1) * LANES]
            if joined:
                out_ref[place + i, 0] = vals
            else:
                out_ref[place + i] = vals


def da_call(given, got, p_own, p_oth, wsh, joined=None):
    rows, dim = given.shape
    pairs = dim // LANES
    arrays = [far(given)] + ([] if got is None else [got])
    arrays += [] if joined is None else [far(joined)]
    shape = (pairs, rows, LANES) if joined is None else (pairs, 2, rows, LANES)
    return local_call(
        functools.partial(da_kernel, got is None),
        "attn_out_backward",
        [wsh],
        arrays,
        [p_own, p_oth],
        [far(shape_of(shape, bf16)), far(shape_of((rows, dim), bf16))],
        half_scratch(p_own),
    )


def dx_kernel(wsh_ref, inputs, weights, outputs, grad_s, buf, sems):
    copies = both_halves(*weights, buf, sems)
    back, dx, sums = outputs
    dqkv_ref, tab_ref = inputs[0].ref(), inputs[1].ref()
    pairs = dqkv_ref.shape[0]
    for part in range(3):
        for pair in range(pairs):
            vals = dqkv_ref[pair, part]
            if part < 2:
                vals = unrope(vals.astype(f32), tab_ref).astype(bf16)
            back.ref[pair, part] = vals
            grad_s[:, pl.ds((part * pairs + pair) * LANES, LANES)] = vals
    back.send()
    vec_ref, x_ref, dy_ref, dnm_ref = (item.ref() for item in inputs[2:])
    first = wsh_ref[0] == 0
    copies[0].wait()
    own = dot_nt(grad_s[...], buf[0])
    copies[1].wait()
    oth = dot_nt(grad_s[...], buf[1])
    dna = jnp.concatenate([jnp.where(first, own, oth), jnp.where(first, oth, own)], axis=1)
    dnm = dnm_ref[...]
    xhat, scale = normalized(x_ref[...].astype(f32))
    grad = dna * vec_ref[0:1] + dnm * vec_ref[2:3]
    inner = (
        grad
        - jnp.mean(grad, axis=-1, keepdims=True)
        - xhat * jnp.mean(grad * xhat, axis=-1, keepdims=True)
    )
    dx.ref[...] = (dy_ref[...].astype(f32) + scale * inner).astype(bf16)
    dx.send()
    sums.ref[0:1] = jnp.sum(dna * xhat, axis=0, keepdims=True)
    sums.ref[1:2] = jnp.sum(dna, axis=0, keepdims=True)
    sums.ref[2:3] = jnp.sum(dnm * xhat, axis=0, keepdims=True)
    sums.ref[3:4] = jnp.sum(dnm, axis=0, keepdims=True)


def dx_call(dqkv, tab, x, dy, dnm, vecs, w_own, w_oth, wsh, after, limit):
    rows, dim = x.shape
    return local_call(
        dx_kernel,
        "section_input_grad",
        [wsh],
        [dqkv, tab, vecs, far(x), far(dy), far(dnm)],
        [w_own, w_oth],
        [far(shape_of(o, t)) for o, t in ((dqkv.shape, bf16), ((rows, dim), bf16), ((4, dim), f32))],
        [pltpu.VMEM((rows, 3 * dim), bf16)] + half_scratch(w_own),
        after,
        limit,
    )


def joined_rows(items):
    return jnp.concatenate([item.ref()[...] for item in items], axis=0)


class Pieces:
    def __init__(self, out_ref, buf, sems):
        self.out_ref, self.buf, self.sems, self.copies = out_ref, buf, sems, []

    def put(self, rows, cols, vals):
        self.buf[rows, cols] = vals.astype(bf16)
        at = len(self.copies)
        self.copies.append(
            pltpu.make_async_copy(
                self.buf.at[rows, cols], self.out_ref.at[rows, cols], self.sems.at[at]
            )
        )
        self.copies[-1].start()

    def finish(self, chunk, ahead, behind):
        height, cut = ahead.ref.shape
        rows = pl.ds(pl.multiple_of(chunk * height, height), height)
        ahead.ref[...] = self.buf[rows, :cut]
        ahead.send()
        behind.ref[...] = self.buf[rows, cut:]
        behind.send()
        wait_all(self.copies)


def grad_call(body, name, idx, arrays, shape, width, count, scratch, after):
    halves = shape_of((shape[0] // count, shape[1] // 2), bf16)
    return local_call(
        functools.partial(body, len(arrays)),
        name,
        [idx],
        arrays,
        [],
        [[shape_of(shape, bf16)], far(halves), far(halves), far(shape_of((1, width), f32))],
        [pltpu.VMEM(shape, bf16), pltpu.SemaphoreType.DMA((4,))] + scratch,
        after,
        TAIL_LIMIT,
    )


def parts_of(items, number):
    size = len(items) // number
    return [items[i * size : (i + 1) * size] for i in range(number)]


def down_grad_kernel(number, idx_ref, inputs, weights, outputs, buf, sems):
    gts, dys = parts_of(inputs, 2)
    out = Pieces(outputs[0].ref, buf, sems)
    dy = joined_rows(dys)
    outputs[3].ref[...] = jnp.sum(dy.astype(f32), axis=0, keepdims=True)
    rows, dim = buf.shape
    tile = rows // 4
    for t in range(4):
        part = slice(t * tile, (t + 1) * tile)
        left = jnp.concatenate([item.ref()[part] for item in gts], axis=1)
        out.put(part, slice(0, dim), dot_nn(left, dy))
    out.finish(idx_ref[idx_ref.shape[0] // 2], outputs[1], outputs[2])


def down_grad_call(idx, gt_list, dy_list, count):
    dim = dy_list[0].shape[1]
    return grad_call(
        down_grad_kernel,
        "down_grad",
        idx,
        [far(a) for a in gt_list + dy_list],
        (gt_list[0].shape[0], dim),
        dim,
        count,
        [],
        [],
    )


def up_grad_kernel(number, idx_ref, inputs, weights, outputs, buf, sems):
    norms, dus = parts_of(inputs, 2)
    out = Pieces(outputs[0].ref, buf, sems)
    left = jnp.concatenate([item.ref()[1] for item in norms], axis=0).T
    rows, ff = buf.shape
    tile = ff // 4
    for t in range(4):
        part = slice(t * tile, (t + 1) * tile)
        du = jnp.concatenate([item.ref()[part] for item in dus], axis=1)
        outputs[3].ref[:, part] = dot_nt(jnp.ones((8, du.shape[1]), bf16), du)[:1]
        out.put(slice(0, rows), part, dot_nt(left, du))
    out.finish(idx_ref[idx_ref.shape[0] // 2], outputs[1], outputs[2])


def up_grad_call(idx, norm_list, du_list, count, after):
    half, ff = norm_list[0].shape[2], du_list[0].shape[0]
    return grad_call(
        up_grad_kernel,
        "up_grad",
        idx,
        [far(a) for a in norm_list + du_list],
        (half, ff),
        ff,
        count,
        [],
        after,
    )


def attn_grad_kernel(number, idx_ref, inputs, weights, outputs, buf, sems):
    norms, outs, dqkvs, dys = parts_of(inputs, 4)
    out = Pieces(outputs[0].ref, buf, sems)
    rows, width = buf.shape
    dim = width // 4
    left = jnp.concatenate([item.ref()[0] for item in norms], axis=0).T
    for part in range(4):
        cols = slice(part * dim, (part + 1) * dim)
        if part < 3:
            right = jnp.concatenate([lanes_of(item.ref().at[:, part]) for item in dqkvs], axis=0)
        else:
            left, right = joined_rows(outs).T, joined_rows(dys)
        outputs[3].ref[:, cols] = jnp.sum(right.astype(f32), axis=0, keepdims=True)
        out.put(slice(0, rows), cols, dot_nn(left, right))
    out.finish(idx_ref[idx_ref.shape[0] // 2], outputs[1], outputs[2])


def attn_grad_call(idx, norm_list, out_list, dqkv_list, dy_list, count, after):
    half, dim = norm_list[0].shape[2], dy_list[0].shape[1]
    return grad_call(
        attn_grad_kernel,
        "attn_grad",
        idx,
        [far(a) for a in norm_list + out_list + dqkv_list + dy_list],
        (half, 4 * dim),
        4 * dim,
        count,
        [],
        after,
    )


def ring_of(count):
    return list(range(0, count, 2)) + list(range(count - 1, 0, -2))


def ring_place(axis):
    count = lax.axis_size(axis)
    me = lax.axis_index(axis)
    return jnp.where(me % 2 == 0, me // 2, count - (me + 1) // 2)


def ring_index(axis):
    count = lax.axis_size(axis)
    return (ring_place(axis) + jnp.arange(count, dtype=jnp.int32)) % count


def ring_shift(vals, axis, by):
    order = ring_of(lax.axis_size(axis))
    count = len(order)
    pairs = [(order[i], order[(i + by) % count]) for i in range(count)]
    return lax.ppermute(vals, axis, pairs)


def tied(token, *vals):
    return lax.optimization_barrier((token, vals))[1]


def fetch(idx_ref, slots, own_ref, bufs, sems):
    return start_all(
        [
            pltpu.make_async_copy(own_ref.at[idx_ref[slot]], bufs.at[i], sems.at[i])
            for i, slot in enumerate(slots)
        ]
    )


def low_total(*terms):
    total = terms[0].astype(f32)
    for term in terms[1:]:
        total = total + term.astype(f32)
    return total.astype(bf16)


def ring_add_kernel(slots, idx_ref, inputs, own_refs, outputs, bufs, sems):
    copies = fetch(idx_ref, slots, own_refs[0], bufs, sems)
    for i, item in enumerate(outputs):
        copies[i].wait()
        got = inputs[i].ref()
        cols, cut = item.ref.shape[1], got.shape[1]
        summed = slice(0, cut) if i == 0 else slice(cols - cut, cols)
        item.ref[:, summed] = low_total(bufs[i, :, summed], got[...])
        if cut < cols:
            rest = slice(cut, cols) if i == 0 else slice(0, cols - cut)
            item.ref[:, rest] = bufs[i, :, rest]
        item.send()


def put_copies(chunk, cols, buf, totals, starts, sem):
    lo, hi = cols, cols + buf.shape[1]
    copies = []
    for i, (total, start) in enumerate(zip(totals, starts)):
        first, last = max(lo, start), min(hi, start + total.shape[2])
        if first < last:
            copies.append(
                pltpu.make_async_copy(
                    buf.at[:, pl.ds(first - lo, last - first)],
                    total.at[chunk, :, pl.ds(first - start, last - first)],
                    sem.at[i],
                )
            )
    return copies


def ring_own_kernel(slots, idx_ref, inputs, own_refs, outputs, bufs, sems):
    wait_all(fetch(idx_ref, slots, own_refs[0], bufs, sems))
    outputs[0].ref[...] = low_total(bufs[0], inputs[0].ref()[...], inputs[1].ref()[...])


def ring_put_kernel(starts, slots, cols, fresh, onward, idx_ref, *refs):
    number = len(slots)
    pieces = refs[:number]
    wide, sems, pass_buf, pass_sems = refs[-4:]
    passed = refs[-4 - onward : -4]
    totals = refs[-4 - onward - len(starts) : -4 - onward]
    leaving = []
    for i, ref in enumerate(passed):
        width = ref.shape[1]
        pass_buf[i, :, :width] = pieces[i][:, :width] if i == 0 else pieces[i][:, -width:]
        leaving += start_all(
            [pltpu.make_async_copy(pass_buf.at[i, :, pl.ds(0, width)], ref, pass_sems.at[i])]
        )
    for i in range(number):
        wide[i] = pieces[i][...].astype(f32)
        leaving += start_all(
            put_copies(idx_ref[slots[i]], cols[i], wide.at[i], totals, starts, sems.at[i])
        )
    wait_all(leaving)


def ring_sum(own, ahead, behind, widths, axis):
    count = lax.axis_size(axis)
    half = count // 2
    full_rows, cols = own.shape
    rows = full_rows // count
    own = own.reshape(count, rows, cols)
    cut = cols // 2
    starts = [sum(widths[:i]) for i in range(len(widths))]
    idx = ring_index(axis)
    chunk, piece = shape_of((rows, cols), bf16), shape_of((rows, cut), bf16)
    sums = [shape_of((count, rows, width), f32) for width in widths]

    def taken(number):
        return [pltpu.VMEM((number, rows, cols), bf16), pltpu.SemaphoreType.DMA((number,))]

    def put(totals, pieces, slots, passed, after):
        number, width = len(pieces), pieces[0].shape[1]
        first_cols = (0,) * number if width == cols else (0, cut)
        fresh = totals is None
        out = pl.pallas_call(
            functools.partial(
                ring_put_kernel,
                starts,
                tuple(k % count for k in slots),
                first_cols,
                fresh,
                len(passed),
            ),
            in_specs=[SCALARS]
            + [HERE] * number
            + [IN_HBM] * (0 if fresh else len(sums))
            + [ANYWHERE] * len(after),
            out_specs=[IN_HBM] * (len(sums) + len(passed)),
            out_shape=sums + passed,
            scratch_shapes=[
                pltpu.VMEM((number, rows, width), f32),
                pltpu.SemaphoreType.DMA((number, len(sums))),
                pltpu.VMEM((2, rows, cols), bf16),
                pltpu.SemaphoreType.DMA((2,)),
            ],
            input_output_aliases={} if fresh else {1 + number + i: i for i in range(len(sums))},
            name="ring_put",
            **params_of(RING_LIMIT),
        )(idx, *pieces, *([] if fresh else totals), *after)
        return out[: len(sums)], out[len(sums) :]

    def both_ways(ahead, behind):
        return ring_shift(ahead, axis, 1), ring_shift(behind, axis, -1)

    token = behind
    ahead, behind = both_ways(ahead, behind)
    token = yield token
    for k in range(half - 1, 0, -1):
        ahead, behind = local_call(
            functools.partial(ring_add_kernel, (k % count, (-k) % count)),
            "ring_add",
            [idx],
            [ahead, behind],
            [own],
            [far(chunk), far(chunk)],
            taken(2),
            [token],
            RING_LIMIT,
        )
        token = behind
        ahead, behind = both_ways(ahead, behind)
        token = yield token
    (mine,) = local_call(
        functools.partial(ring_own_kernel, (0,)),
        "ring_own",
        [idx],
        [ahead, behind],
        [own],
        [far(chunk)],
        taken(1),
        [token],
        RING_LIMIT,
    )
    ahead, behind = both_ways(mine, mine)
    totals, (token,) = put(None, [mine], [0], [shape_of((rows, LANES), bf16)], [])
    token = yield token
    for k in range(1, half):
        passed = [piece if k == half - 1 else chunk] * 2
        totals, passed = put(totals, [ahead, behind], [-k, k], passed, [token])
        token = passed[1]
        ahead, behind = both_ways(*passed)
        token = yield token
    totals, _ = put(totals, [ahead, behind], [-half, half], [], [token])
    yield [total.reshape(full_rows, -1) for total in totals]


def butterfly_sum(vals, axis):
    count = lax.axis_size(axis)
    by = 1
    token = yield None
    if count & (count - 1):
        yield lax.psum(tied(token, vals)[0], axis)
        return
    (vals,) = tied(token, vals)
    while by < count:
        got = lax.ppermute(vals, axis, [(i, i ^ by) for i in range(count)])
        token = yield None
        (got,) = tied(token, got)
        vals = vals + got
        by *= 2
    yield vals


def swap(vals):
    return lax.ppermute(vals, "wsh", [(0, 1), (1, 0)])


def pass_on(vals, by):
    pairs = [(0, 1)] if by > 0 else [(1, 0)]
    return lax.ppermute(vals, "section", pairs)


def block_places(block_pair, count):
    want = jnp.arange(2 * count, dtype=jnp.int32)
    device = jnp.arange(count, dtype=jnp.int32)
    first = (block_pair[None, :] == want[:, None]).astype(jnp.int32)
    second = ((2 * count - 1 - block_pair)[None, :] == want[:, None]).astype(jnp.int32)
    return jnp.sum(first * (2 * device) + second * (2 * device + 1), axis=1)


def row_positions(block_pair, stored, tok_dev):
    count = block_pair.shape[0]
    device = stored // tok_dev
    within = stored % tok_dev
    half_rows = tok_dev // 2
    matches = device[:, None] == jnp.arange(count, dtype=jnp.int32)[None, :]
    pair_block = jnp.sum(jnp.where(matches, block_pair[None, :], 0), axis=1)
    block_idx = jnp.where(within < half_rows, pair_block, 2 * count - 1 - pair_block)
    return block_idx * half_rows + within % half_rows


def rotary_table(positions, head_size):
    half_rot = ROT // 2
    lane = jnp.arange(LANES, dtype=jnp.int32) % head_size
    inv_freq = ROPE_BASE ** (-((lane % half_rot).astype(f32) * 2.0) / ROT)
    angles = positions.astype(f32)[:, None] * inv_freq[None, :]
    cosine, sine = jnp.cos(angles), jnp.sin(angles)
    lead, second = (lane < half_rot)[None], ((lane >= half_rot) & (lane < ROT))[None]
    return jnp.stack(
        [
            jnp.where(lead | second, cosine, 1.0),
            jnp.where(lead, -sine, 0.0),
            jnp.where(second, sine, 0.0),
        ]
    )


def body(
    inputs,
    cotangent,
    block_pair,
    qkv_weight,
    qkv_bias,
    proj_weight,
    proj_bias,
    up_weight,
    up_bias,
    down_weight,
    down_bias,
    attn_gain,
    attn_shift,
    mlp_gain,
    mlp_shift,
):
    first_section = lax.axis_index("section") == 0
    count = lax.axis_size("ctx")
    micros, _, tok_dev, dim = inputs.shape
    head_size = dim // HEADS
    half = dim // 2
    my_half = lax.axis_index("wsh")
    wsh = jnp.stack([my_half.astype(jnp.int32), first_section.astype(jnp.int32)])
    one_pair_each = count == dim // LANES

    wq, wp, wu, wd = (w[0] for w in (qkv_weight, proj_weight, up_weight, down_weight))
    small = jnp.concatenate(
        [
            v[0].reshape(-1, half)
            for v in (
                attn_gain,
                attn_shift,
                mlp_gain,
                mlp_shift,
                proj_bias,
                down_bias,
                qkv_bias,
                up_bias,
            )
        ],
        axis=0,
    )
    small_oth = swap(small)
    wq_oth = swap(wq)
    first_here = lax.optimization_barrier((wq_oth, small_oth))
    wq_oth, small_oth = first_here
    wu_oth = swap(tied(wq_oth, wu)[0])
    wd_oth = swap(tied(wq_oth, wd)[0])
    wp_oth = swap(tied(wu_oth, wp)[0])
    low_part = jnp.where(my_half == 0, small, small_oth).astype(f32)
    high_part = jnp.where(my_half == 0, small_oth, small).astype(f32)
    vecs = jnp.concatenate([low_part[:6], high_part[:6]], axis=1)
    qkv_rows = 6 + qkv_bias.shape[1] // half
    proj_b, down_b = vecs[4:5], vecs[5:6]
    qkv_b = jnp.concatenate([low_part[6:qkv_rows], high_part[6:qkv_rows]], axis=0).reshape(1, -1)
    up_b = jnp.concatenate([low_part[qkv_rows:], high_part[qkv_rows:]], axis=0).reshape(1, -1)

    local_rows = lax.axis_index("ctx") * tok_dev + jnp.arange(tok_dev, dtype=jnp.int32)
    query_pos = row_positions(block_pair, local_rows, tok_dev)
    key_pos = row_positions(block_pair, jnp.arange(count * tok_dev, dtype=jnp.int32), tok_dev)
    tab = rotary_table(query_pos, head_size)
    loc = block_places(block_pair, count)

    def exchange(vals):
        return lax.all_to_all(vals, "ctx", split_axis=0, concat_axis=0, tiled=True)

    rows_in = [inputs[i, 0] for i in range(micros)]
    cot_in = [cotangent[i, 0] for i in range(micros)]

    def norm_qkv(index, got):
        return qkv_call(rows_in[index], got, vecs, qkv_b, tab, wq, wq_oth, wsh)

    def mlp(made, save):
        return mlp_call(made[2], made[3], up_b, down_b, wu, wu_oth, wd, wd_oth, wsh, save)

    def mlp_back(dy, mlp_kept, after=(), limit=VMEM_LIMIT):
        return mlp_back_call(dy, mlp_kept[1], wu, wu_oth, wd, wd_oth, wsh, after, limit)

    def out_back(index, got, joined=None):
        return da_call(cot_in[index], got, wp, wp_oth, wsh, joined)

    def moved(vals):
        return exchange(vals) if one_pair_each else vals

    def attend(qkv, after=()):
        if one_pair_each:
            attended, lse = attend_call(qkv, loc, after)
            return attended, (qkv, lse)
        return wide_attend(qkv, query_pos, key_pos)

    def attend_back(kept, da, after=(), limit=VMEM_LIMIT):
        if one_pair_each:
            return attend_back_call(kept[0], da, kept[1], loc, after, limit)
        da = da[:, 0] if da.ndim == 4 else da
        return wide_attend_back(kept, da, query_pos, key_pos)

    def project(attended, made, mlp_out, after=(), limit=VMEM_LIMIT):
        return proj_call(attended, made[1], mlp_out[0], proj_b, wp, wp_oth, wsh, after, limit)

    def input_grad_of(dqkv, made, dy, dnm, after=(), limit=VMEM_LIMIT):
        return dx_call(dqkv, tab, made[1], dy, dnm, vecs, wq, wq_oth, wsh, after, limit)

    made_a = norm_qkv(0, None)
    qkv_a = moved(made_a[0])
    mlp_a = mlp(made_a, False)
    att_a, _ = attend(qkv_a, [mlp_a[0]])
    att_a = moved(att_a)
    da_a, dy_a = out_back(0, None)
    y_a = project(att_a, made_a, mlp_a, [dy_a])[0]
    da_a = moved(tied(y_a, da_a)[0])

    made_b = norm_qkv(1, pass_on(y_a, 1))
    qkv_2 = moved(tied(da_a, made_b[0])[0])
    norms_b = swap(made_b[3])
    mlp_b = mlp(made_b, True)
    att_b, kept_b = attend(qkv_2, [mlp_b[0], norms_b])
    att_b = moved(att_b)
    gt_b = swap(mlp_b[3])
    dqkv_a_ = attend_back(kept_b, da_a, [gt_b])
    dqkv_a = moved(dqkv_a_)
    y_b, *a_b = project(att_b, made_b, mlp_b, [dqkv_a_])

    made_c = norm_qkv(0, pass_on(y_b, 1))
    qkv_3 = moved(tied(dqkv_a, made_c[0])[0])
    norms_c = swap(made_c[3])
    a_b_oth = swap(a_b[1])
    _, dnm_a = mlp_back(dy_a, mlp_b, [made_c[1]])
    _, dx_a, _ = input_grad_of(dqkv_a, made_b, dy_a, dnm_a, [norms_c, a_b_oth])
    got_a = pass_on(dx_a, -1)
    mlp_c = mlp_call(
        made_c[2], tied(dx_a, made_c[3])[0], up_b, down_b, wu, wu_oth, wd, wd_oth, wsh, True
    )
    da_b, dy_b = out_back(1, tied(mlp_c[0], got_a)[0])
    da_b = moved(tied(qkv_3, da_b)[0])
    att_c, kept_c = attend(qkv_3, [dy_b])
    dy_b_oth, gt_c = swap(dy_b), swap(mlp_c[3])
    dqkv_b = attend_back(kept_c, da_b, [dy_b_oth, gt_c])
    dqkv_b_ = moved(dqkv_b)
    du_b, dnm_b = mlp_back(dy_b, mlp_c, [dqkv_b])
    du_b_oth = swap(du_b)
    back_b, dx_b, sums_b = input_grad_of(dqkv_b_, made_c, dy_b, dnm_b, [du_b_oth])
    got_b = pass_on(dx_b, -1)
    back_b_oth = swap(back_b)

    da_c, dy_c = out_back(0, tied(back_b_oth, got_b)[0], att_c if one_pair_each else None)
    dy_list = [dy_c, dy_b, swap(dy_c), dy_b_oth]
    da_c = moved(da_c)
    idx = ring_index("ctx")
    *down_made, dy_sum = down_grad_call(idx, [mlp_b[2], mlp_c[2], gt_b, gt_c], dy_list, count)
    down_ring = ring_sum(*down_made, (dim,), "ctx")
    token = next(down_ring)
    token = down_ring.send(token)
    du_c, dnm_c = mlp_back(dy_c, mlp_b, [token], TAIL_LIMIT)
    dqkv_c = attend_back(kept_b, da_c, [dnm_c], TAIL_LIMIT)
    token = down_ring.send(dqkv_c)
    dqkv_c = moved(dqkv_c)
    *up_made, du_sum = up_grad_call(
        idx,
        [made_b[2], made_c[2], norms_b, norms_c],
        [du_c, du_b, swap(du_c), du_b_oth],
        count,
        [token],
    )
    up_ring = ring_sum(*up_made, (up_made[0].shape[1],), "ctx")
    token = next(up_ring)
    steps = count + 1
    left = {down_ring: steps - 3, up_ring: steps - 1}
    results = {}

    def turn(ring, token):
        if not left[ring]:
            return token
        left[ring] -= 1
        made = ring.send(token)
        if left[ring] == 0:
            results[ring] = made
            return token
        return made

    token = turn(down_ring, token)
    token = turn(up_ring, token)
    back_c, dx_c, sums_c = input_grad_of(dqkv_c, made_b, dy_c, dnm_c, [token], TAIL_LIMIT)
    back_c_oth = swap(back_c)
    token = turn(down_ring, dx_c)
    y_c, *a_c = project(da_c if one_pair_each else att_c, made_c, mlp_c, [token], TAIL_LIMIT)
    a_c_oth = swap(a_c[1])
    token = turn(up_ring, y_c)
    token = turn(down_ring, token)
    *attn_made, attn_sum = attn_grad_call(
        idx,
        [made_b[2], made_c[2], norms_b, norms_c],
        [a_b[0], a_c[0], a_b_oth, a_c_oth],
        [back_c, back_b, back_c_oth, back_b_oth],
        dy_list,
        count,
        [token],
    )
    dqkv_sum = attn_sum[:, : 3 * dim]
    attn_ring = ring_sum(*attn_made, (3 * dim, dim), "ctx")
    token = next(attn_ring)
    left[attn_ring] = steps - 1

    norm_sums = sums_b + sums_c
    norm_own = lax.dynamic_slice_in_dim(norm_sums, my_half * half, half, 1)
    norm_oth = swap(lax.dynamic_slice_in_dim(norm_sums, (1 - my_half) * half, half, 1))

    def own_part(vec):
        size = vec.shape[1] // 2
        return lax.dynamic_slice_in_dim(vec, my_half * size, size, 1).reshape(-1, half)

    (norm_oth,) = tied(token, norm_oth)
    small_sums = jnp.concatenate(
        [norm_own + norm_oth, own_part(dy_sum), own_part(dqkv_sum), own_part(du_sum)], axis=0
    )
    small_ring = butterfly_sum(small_sums, "ctx")
    next(small_ring)
    at = 0
    summed = None
    while any(left.values()):
        token = turn((up_ring, attn_ring, down_ring, attn_ring)[at % 4], token)
        if at % 2 == 0 and summed is None:
            summed = small_ring.send(token)
        at += 1
    while summed is None:
        summed = small_ring.send(token)
    small_sums = summed
    (down_grad,) = results[down_ring]
    (up_grad,) = results[up_ring]
    qkv_grad, proj_grad = results[attn_ring]

    qkv_end = 5 + dqkv_sum.shape[1] // 2 // half
    dy_total = small_sums[4:5]
    pick = lambda yes, no: jnp.where(first_section, yes, no)
    layer_out = jnp.stack([pick(y_c, y_b), pick(y_b, y_c)])[None, :, None]
    input_grad = jnp.stack([pick(dx_b, dx_c), pick(dx_c, dx_b)])[None, :, None]
    return (
        layer_out,
        input_grad,
        qkv_grad[None],
        small_sums[5:qkv_end].reshape(1, -1),
        proj_grad[None],
        dy_total,
        up_grad[None],
        small_sums[qkv_end:].reshape(1, -1),
        down_grad[None],
        dy_total,
        small_sums[0:1],
        small_sums[1:2],
        small_sums[2:3],
        small_sums[3:4],
    )


def solution(mesh):
    in_specs = (
        P(None, "wsh", "ctx", None),
        P(None, "wsh", "ctx", None),
        P(),
        P("section", "wsh", None),
        P("section", "wsh"),
        P("section", "wsh", None),
        P("section", "wsh"),
        P("section", "wsh", None),
        P("section", "wsh"),
        P("section", "wsh", None),
        P("section", "wsh"),
        P("section", "wsh"),
        P("section", "wsh"),
        P("section", "wsh"),
        P("section", "wsh"),
    )
    out_specs = (
        P("section", None, "wsh", "ctx", None),
        P("section", None, "wsh", "ctx", None),
        P("section", "wsh", None),
        P("section", "wsh"),
        P("section", "wsh", None),
        P("section", "wsh"),
        P("section", "wsh", None),
        P("section", "wsh"),
        P("section", "wsh", None),
        P("section", "wsh"),
        P("section", "wsh"),
        P("section", "wsh"),
        P("section", "wsh"),
        P("section", "wsh"),
    )
    return jax.shard_map(body, mesh=mesh, in_specs=in_specs, out_specs=out_specs, check_vma=False)
```

profile of v0, /device:TPU:0, one launch (start us, length us, event | category | flops | bytes accessed | tf_op | source)
XLA Modules:
  0.0 609.8 jit_solution(15723306452816937404)
XLA Ops:
  18.8 7.2 %all-to-all-start = ((bf16[8,3,128,128]{3,2,1,0:T(8,128)(2,1)}), bf16[8,3,128,128]{3,2,1,0:T(8,128)(2,1)S(1)}, u32[]{:S(2)}, u32[]{:S(2)}) async-start(bf16[8,3,128,128]{3,2,1,0:T(8,128)(2,1)} %get-tuple-element.152), calls=%async_computation | async-start | bytes 1572864 | tf_op jit(solution)/shard_map/all_to_all | solution.py:1202
  28.0 11.0 %mlp_forward.3.refs_2_.refs_4_ = f32[128,1024]{1,0:T(8,128)} custom-call(s32[2]{0:T(128)} %pad_add_fusion.refs_0_, bf16[2,128,512]{2,1,0:T(8,128)(2,1)} %get-tuple-element.153.refs_1_, bf16[2,128,512]{2,1,0:T(8,128)(2,1)} %get-tuple-element.154.refs_2_, f32[1,4096]{1,0:T(1,128)} %bitcast.97, f32[1,1024]{1,0:T(1,128)} %get-tuple-element.328.refs_4_, ...), custom_call_target="tpu_custom_call" | custom-call | flops 1 | bytes 1 | tf_op jit(solution)/shard_map/mlp_forward/pallas_call | solution.py:210
  39.0 7.5 %all-to-all-done.refs_1_ = bf16[8,3,128,128]{3,2,1,0:T(8,128)(2,1)S(1)} async-done(((bf16[8,3,128,128]{3,2,1,0:T(8,128)(2,1)}), bf16[8,3,128,128]{3,2,1,0:T(8,128)(2,1)S(1)}, u32[]{:S(2)}, u32[]{:S(2)}) %all-to-all-start) | async-done | bytes 786464 | tf_op jit(solution)/shard_map/all_to_all | solution.py:1202
  96.1 11.7 %mlp_forward.4 = (f32[128,1024]{1,0:T(8,128)}, bf16[4096,128]{1,0:T(8,128)(2,1)}, bf16[2048,128]{1,0:T(8,128)(2,1)}, bf16[2048,128]{1,0:T(8,128)(2,1)}) custom-call(s32[2]{0:T(128)} %pad_add_fusion.refs_0_, bf16[2,128,512]{2,1,0:T(8,128)(2,1)} %get-tuple-element.166.refs_1_, bf16[2,128,512]{2,1,0:T(8,128)(2,1)} %get-tuple-element.167.refs_2_, ...), custom_call_target="tpu_custom_call" | custom-call | flops 1 | bytes 1 | tf_op jit(solution)/shard_map/mlp_forward/pallas_call | solution.py:210
  125.9 8.7 %attention_backward.3.refs_7_ = bf16[8,3,128,128]{3,2,1,0:T(8,128)(2,1)} custom-call(s32[16]{0:T(128)} %add_reduce_fusion.refs_0_, bf16[8,128,128]{2,1,0:T(8,128)(2,1)} %copy-done.38, bf16[8,3,128,128]{3,2,1,0:T(8,128)(2,1)} %copy-done.22, f32[2,1024]{1,0:T(2,128)} %get-tuple-element.169.refs_3_, bf16[2048,128]{1,0:T(8,128)(2,1)} %copy-done.32), custom_call_target="tpu_custom_call" | custom-call | flops 1 | bytes 1 | tf_op jit(solution)/shard_map/attention_backward/pallas_call | solution.py:210
  167.6 14.3 %mlp_backward.3 = (bf16[4096,128]{1,0:T(8,128)(2,1)}, f32[128,1024]{1,0:T(8,128)}) custom-call(s32[2]{0:T(128)} %pad_add_fusion.refs_0_, bf16[128,1024]{1,0:T(8,128)(2,1)} %get-tuple-element.160.refs_7_.refs_1_.refs_5_, bf16[4096,128]{1,0:T(8,128)(2,1)} %get-tuple-element.177.refs_2_, bf16[512,4096]{1,0:T(8,128)(2,1)} %bitcast.56, ...), custom_call_target="tpu_custom_call" | custom-call | flops 1 | bytes 1 | tf_op jit(solution)/shard_map/mlp_backward/pallas_call | solution.py:210
  182.7 7.1 %section_input_grad.3 = (bf16[8,3,128,128]{3,2,1,0:T(8,128)(2,1)}, bf16[128,1024]{1,0:T(8,128)(2,1)}, f32[4,1024]{1,0:T(4,128)}) custom-call(s32[2]{0:T(128)} %pad_add_fusion.refs_0_, bf16[8,3,128,128]{3,2,1,0:T(8,128)(2,1)} %copy-done.26, f32[3,128,128]{2,1,0:T(8,128)} %pad_maximum_fusion.refs_4_.refs_2_, f32[6,1024]{1,0:T(8,128)} %pad_maximum_fusion.1.refs_2_.refs_3_, ...), custom_call_target="tpu_custom_call" | custom-call | flops 1 | bytes 1 | tf_op jit(solution)/shard_map/section_input_grad/pallas_call | solution.py:210
  191.1 11.8 %mlp_forward.5 = (f32[128,1024]{1,0:T(8,128)}, bf16[4096,128]{1,0:T(8,128)(2,1)}, bf16[2048,128]{1,0:T(8,128)(2,1)}, bf16[2048,128]{1,0:T(8,128)(2,1)}) custom-call(s32[2]{0:T(128)} %pad_add_fusion.refs_0_, bf16[2,128,512]{2,1,0:T(8,128)(2,1)} %get-tuple-element.176.refs_1_.refs_2_, bf16[2,128,512]{2,1,0:T(8,128)(2,1)} %get-tuple-element.183.refs_2_, ...), custom_call_target="tpu_custom_call" | custom-call | flops 1 | bytes 1 | tf_op jit(solution)/shard_map/mlp_forward/pallas_call | solution.py:210
  224.2 8.7 %attention_backward.4.refs_7_ = bf16[8,3,128,128]{3,2,1,0:T(8,128)(2,1)} custom-call(s32[16]{0:T(128)} %add_reduce_fusion.refs_0_, bf16[8,128,128]{2,1,0:T(8,128)(2,1)} %copy-done.36, bf16[8,3,128,128]{3,2,1,0:T(8,128)(2,1)} %copy-done.23, f32[2,1024]{1,0:T(2,128)} %get-tuple-element.189.refs_3_, bf16[128,1024]{1,0:T(8,128)(2,1)} %copy-done.31, ...), custom_call_target="tpu_custom_call" | custom-call | flops 1 | bytes 1 | tf_op jit(solution)/shard_map/attention_backward/pallas_call | solution.py:210
  237.0 14.4 %mlp_backward.4 = (bf16[4096,128]{1,0:T(8,128)(2,1)}, f32[128,1024]{1,0:T(8,128)}) custom-call(s32[2]{0:T(128)} %pad_add_fusion.refs_0_, bf16[128,1024]{1,0:T(8,128)(2,1)} %get-tuple-element.188.refs_2_.refs_1_.refs_5_.refs_6_.refs_14_, bf16[4096,128]{1,0:T(8,128)(2,1)} %get-tuple-element.191.refs_2_, bf16[512,4096]{1,0:T(8,128)(2,1)} %bitcast.58, ...), custom_call_target="tpu_custom_call" | custom-call | flops 1 | bytes 1 | tf_op jit(solution)/shard_map/mlp_backward/pallas_call | solution.py:210
  258.2 7.1 %section_input_grad.4 = (bf16[8,3,128,128]{3,2,1,0:T(8,128)(2,1)}, bf16[128,1024]{1,0:T(8,128)(2,1)}, f32[4,1024]{1,0:T(4,128)}) custom-call(s32[2]{0:T(128)} %pad_add_fusion.refs_0_, bf16[8,3,128,128]{3,2,1,0:T(8,128)(2,1)} %copy-done.27, f32[3,128,128]{2,1,0:T(8,128)} %pad_maximum_fusion.refs_4_.refs_2_, f32[6,1024]{1,0:T(8,128)} %pad_maximum_fusion.1.refs_2_.refs_3_, ...), custom_call_target="tpu_custom_call" | custom-call | flops 1 | bytes 1 | tf_op jit(solution)/shard_map/section_input_grad/pallas_call | solution.py:210
  266.7 9.8 %collective-permute-done.16.refs_2_ = bf16[128,1024]{1,0:T(8,128)(2,1)S(1)} collective-permute-done((bf16[128,1024]{1,0:T(8,128)(2,1)}, bf16[128,1024]{1,0:T(8,128)(2,1)S(1)}, u32[]{:S(2)}, u32[]{:S(2)}) %collective-permute-start.16) | collective-permute-done | bytes 262176 | tf_op jit(solution)/shard_map/ppermute | solution.py:1099
  296.3 7.3 %collective-permute-done.18.refs_1_ = bf16[256,512]{1,0:T(8,128)(2,1)S(1)} collective-permute-done((bf16[256,512]{1,0:T(8,128)(2,1)}, bf16[256,512]{1,0:T(8,128)(2,1)S(1)}, u32[]{:S(2)}, u32[]{:S(2)}) %collective-permute-start.18) | collective-permute-done | bytes 262176 | tf_op jit(solution)/shard_map/ppermute | solution.py:906
  311.0 14.3 %mlp_backward.5 = (bf16[4096,128]{1,0:T(8,128)(2,1)}, f32[128,1024]{1,0:T(8,128)}) custom-call(s32[2]{0:T(128)} %pad_add_fusion.refs_0_, bf16[128,1024]{1,0:T(8,128)(2,1)} %get-tuple-element.201.refs_5_.refs_1_.refs_13_, bf16[4096,128]{1,0:T(8,128)(2,1)} %get-tuple-element.177.refs_2_, bf16[512,4096]{1,0:T(8,128)(2,1)} %bitcast.59, ...), custom_call_target="tpu_custom_call" | custom-call | flops 1 | bytes 1 | tf_op jit(solution)/shard_map/mlp_backward/pallas_call | solution.py:210
  326.2 8.8 %attention_backward.5.refs_4_ = bf16[8,3,128,128]{3,2,1,0:T(8,128)(2,1)} custom-call(s32[16]{0:T(128)} %add_reduce_fusion.refs_0_, bf16[8,2,128,128]{3,2,1,0:T(8,128)(2,1)} %copy-done.24, bf16[8,3,128,128]{3,2,1,0:T(8,128)(2,1)} %copy-done.22, f32[2,1024]{1,0:T(2,128)} %get-tuple-element.169.refs_3_, f32[128,1024]{1,0:T(8,128)} %get-tuple-element.207.refs_4_.refs_6_), custom_call_target="tpu_custom_call" | custom-call | flops 1 | bytes 1 | tf_op jit(solution)/shard_map/attention_backward/pallas_call | solution.py:210
  344.7 8.4 %up_grad.1 = (bf16[512,4096]{1,0:T(8,128)(2,1)}, bf16[64,2048]{1,0:T(8,128)(2,1)}, bf16[64,2048]{1,0:T(8,128)(2,1)}, f32[1,4096]{1,0:T(1,128)}) custom-call(s32[8]{0:T(128)} %and_select_fusion.refs_0_.idx_ref, bf16[2,128,512]{2,1,0:T(8,128)(2,1)} %get-tuple-element.166.refs_1_, bf16[2,128,512]{2,1,0:T(8,128)(2,1)} %get-tuple-element.176.refs_1_.refs_2_, ...), custom_call_target="tpu_custom_call" | custom-call | flops 1 | bytes 1 | tf_op jit(solution)/shard_map/up_grad/pallas_call | solution.py:210
  353.1 12.0 %collective-permute-done.22.refs_1_ = bf16[256,1024]{1,0:T(8,128)(2,1)S(1)} collective-permute-done((bf16[256,1024]{1,0:T(8,128)(2,1)S(1)}, bf16[256,1024]{1,0:T(8,128)(2,1)S(1)}, u32[]{:S(2)}, u32[]{:S(2)}) %collective-permute-start.22) | collective-permute-done | bytes 524320 | tf_op jit(solution)/shard_map/ppermute | solution.py:906
  377.8 15.0 %collective-permute-done.27.refs_1_ = bf16[64,2048]{1,0:T(8,128)(2,1)S(1)} collective-permute-done((bf16[64,2048]{1,0:T(8,128)(2,1)}, bf16[64,2048]{1,0:T(8,128)(2,1)S(1)}, u32[]{:S(2)}, u32[]{:S(2)}) %collective-permute-start.27) | collective-permute-done | bytes 262176 | tf_op jit(solution)/shard_map/ppermute | solution.py:906
  399.3 7.1 %section_input_grad.5 = (bf16[8,3,128,128]{3,2,1,0:T(8,128)(2,1)}, bf16[128,1024]{1,0:T(8,128)(2,1)}, f32[4,1024]{1,0:T(4,128)}) custom-call(s32[2]{0:T(128)} %pad_add_fusion.refs_0_, bf16[8,3,128,128]{3,2,1,0:T(8,128)(2,1)} %all-to-all-done.10.refs_1_, f32[3,128,128]{2,1,0:T(8,128)} %pad_maximum_fusion.refs_4_.refs_2_, ...), custom_call_target="tpu_custom_call" | custom-call | flops 1 | bytes 1 | tf_op jit(solution)/shard_map/section_input_grad/pallas_call | solution.py:210
  427.6 7.6 %attn_grad.1 = (bf16[512,4096]{1,0:T(8,128)(2,1)}, bf16[64,2048]{1,0:T(8,128)(2,1)}, bf16[64,2048]{1,0:T(8,128)(2,1)}, f32[1,4096]{1,0:T(1,128)}) custom-call(s32[8]{0:T(128)} %and_select_fusion.refs_0_.idx_ref, bf16[2,128,512]{2,1,0:T(8,128)(2,1)} %get-tuple-element.166.refs_1_, bf16[2,128,512]{2,1,0:T(8,128)(2,1)} %get-tuple-element.176.refs_1_.refs_2_, ...), custom_call_target="tpu_custom_call" | custom-call | flops 1 | bytes 1 | tf_op jit(solution)/shard_map/attn_grad/pallas_call | solution.py:210
  504.8 7.2 %collective-permute-done.47.refs_1_ = bf16[64,4096]{1,0:T(8,128)(2,1)S(1)} collective-permute-done((bf16[64,4096]{1,0:T(8,128)(2,1)S(1)}, bf16[64,4096]{1,0:T(8,128)(2,1)S(1)}, u32[]{:S(2)}, u32[]{:S(2)}) %collective-permute-start.47) | collective-permute-done | bytes 524320 | tf_op jit(solution)/shard_map/ppermute | solution.py:906
  529.5 7.0 %collective-permute-done.52.refs_1_ = bf16[64,4096]{1,0:T(8,128)(2,1)S(1)} collective-permute-done((bf16[64,4096]{1,0:T(8,128)(2,1)S(1)}, bf16[64,4096]{1,0:T(8,128)(2,1)S(1)}, u32[]{:S(2)}, u32[]{:S(2)}) %collective-permute-start.52) | collective-permute-done | bytes 524320 | tf_op jit(solution)/shard_map/ppermute | solution.py:906
  541.1 15.9 %collective-permute-done.64 = f32[12,512]{1,0:T(8,128)S(1)} collective-permute-done((f32[12,512]{1,0:T(8,128)S(1)}, f32[12,512]{1,0:T(8,128)S(1)}, u32[]{:S(2)}, u32[]{:S(2)}) %collective-permute-start.64) | collective-permute-done | bytes 24608 | tf_op jit(solution)/shard_map/ppermute | solution.py:1085
  570.0 17.6 %collective-permute-done.66 = f32[12,512]{1,0:T(8,128)S(1)} collective-permute-done((f32[12,512]{1,0:T(8,128)S(1)}, f32[12,512]{1,0:T(8,128)S(1)}, u32[]{:S(2)}, u32[]{:S(2)}) %collective-permute-start.66) | collective-permute-done | bytes 24608 | tf_op jit(solution)/shard_map/ppermute | solution.py:1085
  (366 shorter events, 360.0 us)
Async XLA Ops:
  18.8 27.7 %all-to-all-start = ((bf16[8,3,128,128]{3,2,1,0:T(8,128)(2,1)}), bf16[8,3,128,128]{3,2,1,0:T(8,128)(2,1)S(1)}, u32[]{:S(2)}, u32[]{:S(2)}) async-start(bf16[8,3,128,128]{3,2,1,0:T(8,128)(2,1)} %get-tuple-element.152), calls=%async_computation | async-start | bytes 1572864 | tf_op jit(solution)/shard_map/all_to_all | solution.py:1202
  26.1 31.5 %collective-permute-start.4 = (bf16[512,1024]{1,0:T(8,128)(2,1)}, bf16[512,1024]{1,0:T(8,128)(2,1)S(1)}, u32[]{:S(2)}, u32[]{:S(2)}) collective-permute-start(bf16[512,1024]{1,0:T(8,128)(2,1)} %bitcast.89), channel_id=1, source_target_pairs={{0,1},{1,0},{2,3},{3,2},{4,5},{5,4},{6,7},{7,6},{8,9},{9,8},{10,11... | collective-permute-start | bytes 3145736 | tf_op jit(solution)/shard_map/ppermute | solution.py:1094
  90.3 24.1 %all-to-all-start.3 = ((bf16[8,3,128,128]{3,2,1,0:T(8,128)(2,1)}), bf16[8,3,128,128]{3,2,1,0:T(8,128)(2,1)S(1)}, u32[]{:S(2)}, u32[]{:S(2)}) async-start(bf16[8,3,128,128]{3,2,1,0:T(8,128)(2,1)} %get-tuple-element.165), calls=%async_computation.3 | async-start | bytes 1572864 | tf_op jit(solution)/shard_map/all_to_all | solution.py:1202
  134.6 26.2 %all-to-all-start.4 = ((bf16[8,3,128,128]{3,2,1,0:T(8,128)(2,1)}), bf16[8,3,128,128]{3,2,1,0:T(8,128)(2,1)S(1)}, u32[]{:S(2)}, u32[]{:S(2)}) async-start(bf16[8,3,128,128]{3,2,1,0:T(8,128)(2,1)} %attention_backward.3.refs_7_), calls=%async_computation.4 | async-start | bytes 1572864 | tf_op jit(solution)/shard_map/all_to_all | solution.py:1202
  160.8 47.0 %all-to-all-start.6 = ((bf16[8,3,128,128]{3,2,1,0:T(8,128)(2,1)}), bf16[8,3,128,128]{3,2,1,0:T(8,128)(2,1)S(1)}, u32[]{:S(2)}, u32[]{:S(2)}) async-start(bf16[8,3,128,128]{3,2,1,0:T(8,128)(2,1)} %get-tuple-element.175), calls=%async_computation.6 | async-start | bytes 1572864 | tf_op jit(solution)/shard_map/all_to_all | solution.py:1202
  232.9 24.4 %all-to-all-start.8 = ((bf16[8,3,128,128]{3,2,1,0:T(8,128)(2,1)}), bf16[8,3,128,128]{3,2,1,0:T(8,128)(2,1)S(1)}, u32[]{:S(2)}, u32[]{:S(2)}) async-start(bf16[8,3,128,128]{3,2,1,0:T(8,128)(2,1)} %attention_backward.4.refs_7_), calls=%async_computation.8 | async-start | bytes 1572864 | tf_op jit(solution)/shard_map/all_to_all | solution.py:1202
  281.4 44.1 %all-to-all-start.9 = ((bf16[8,2,128,128]{3,2,1,0:T(8,128)(2,1)}), bf16[8,2,128,128]{3,2,1,0:T(8,128)(2,1)S(1)}, u32[]{:S(2)}, u32[]{:S(2)}) async-start(bf16[8,2,128,128]{3,2,1,0:T(8,128)(2,1)} %get-tuple-element.198), calls=%async_computation.9 | async-start | bytes 1048576 | tf_op jit(solution)/shard_map/all_to_all | solution.py:1202
  308.8 30.5 %collective-permute-start.20 = (bf16[256,1024]{1,0:T(8,128)(2,1)S(1)}, bf16[256,1024]{1,0:T(8,128)(2,1)S(1)}, u32[]{:S(2)}, u32[]{:S(2)}) collective-permute-start(bf16[256,1024]{1,0:T(8,128)(2,1)S(1)} %get-tuple-element.205), channel_id=1, source_target_pairs={{0,4},{4,8},{8,12},{12,14},{14,10},{10,6},{6,2},{2,0},{1,5},{5,9},... | collective-permute-start | bytes 1572872 | tf_op jit(solution)/shard_map/ppermute | solution.py:906
  309.6 29.7 %collective-permute-start.21 = (bf16[256,1024]{1,0:T(8,128)(2,1)S(1)}, bf16[256,1024]{1,0:T(8,128)(2,1)S(1)}, u32[]{:S(2)}, u32[]{:S(2)}) collective-permute-start(bf16[256,1024]{1,0:T(8,128)(2,1)S(1)} %get-tuple-element.206.refs_7_), channel_id=1, source_target_pairs={{0,2},{4,0},{8,4},{12,8},{14,12},{10,14},{6,10},{2,6},{1,3},{5,1},... | collective-permute-start | bytes 1572872 | tf_op jit(solution)/shard_map/ppermute | solution.py:906
  335.0 64.2 %all-to-all-start.10 = ((bf16[8,3,128,128]{3,2,1,0:T(8,128)(2,1)}), bf16[8,3,128,128]{3,2,1,0:T(8,128)(2,1)}, u32[]{:S(2)}, u32[]{:S(2)}) async-start(bf16[8,3,128,128]{3,2,1,0:T(8,128)(2,1)} %attention_backward.5.refs_4_), calls=%async_computation.10 | async-start | bytes 1572864 | tf_op jit(solution)/shard_map/all_to_all | solution.py:1202
  342.5 22.7 %collective-permute-start.22 = (bf16[256,1024]{1,0:T(8,128)(2,1)S(1)}, bf16[256,1024]{1,0:T(8,128)(2,1)S(1)}, u32[]{:S(2)}, u32[]{:S(2)}) collective-permute-start(bf16[256,1024]{1,0:T(8,128)(2,1)S(1)} %get-tuple-element.208), channel_id=1, source_target_pairs={{0,4},{4,8},{8,12},{12,14},{14,10},{10,6},{6,2},{2,0},{1,5},{5,9},... | collective-permute-start | bytes 1572872 | tf_op jit(solution)/shard_map/ppermute | solution.py:906
  370.0 36.5 %collective-permute-start.25 = (bf16[256,1024]{1,0:T(8,128)(2,1)}, bf16[256,1024]{1,0:T(8,128)(2,1)S(1)}, u32[]{:S(2)}, u32[]{:S(2)}) collective-permute-start(bf16[256,1024]{1,0:T(8,128)(2,1)} %get-tuple-element.212), channel_id=1, source_target_pairs={{0,4},{4,8},{8,12},{12,14},{14,10},{10,6},{6,2},{2,0},{1,5},{5,9},... | collective-permute-start | bytes 1572872 | tf_op jit(solution)/shard_map/ppermute | solution.py:906
  375.8 30.7 %collective-permute-start.26 = (bf16[256,1024]{1,0:T(8,128)(2,1)S(1)}, bf16[256,1024]{1,0:T(8,128)(2,1)S(1)}, u32[]{:S(2)}, u32[]{:S(2)}) collective-permute-start(bf16[256,1024]{1,0:T(8,128)(2,1)S(1)} %get-tuple-element.213.refs_4_), channel_id=1, source_target_pairs={{0,2},{4,0},{8,4},{12,8},{14,12},{10,14},{6,10},{2,6},{1,3},{5,1},... | collective-permute-start | bytes 1572872 | tf_op jit(solution)/shard_map/ppermute | solution.py:906
  450.6 29.7 %collective-permute-start.46 = (bf16[64,4096]{1,0:T(8,128)(2,1)S(1)}, bf16[64,4096]{1,0:T(8,128)(2,1)S(1)}, u32[]{:S(2)}, u32[]{:S(2)}) collective-permute-start(bf16[64,4096]{1,0:T(8,128)(2,1)S(1)} %get-tuple-element.232.refs_4_), channel_id=1, source_target_pairs={{0,2},{4,0},{8,4},{12,8},{14,12},{10,14},{6,10},{2,6},{1,3},{5,1},... | collective-permute-start | bytes 1572872 | tf_op jit(solution)/shard_map/ppermute | solution.py:906
  455.9 22.5 %collective-permute-start.45 = (bf16[64,4096]{1,0:T(8,128)(2,1)S(1)}, bf16[64,4096]{1,0:T(8,128)(2,1)S(1)}, u32[]{:S(2)}, u32[]{:S(2)}) collective-permute-start(bf16[64,4096]{1,0:T(8,128)(2,1)S(1)} %get-tuple-element.240), channel_id=1, source_target_pairs={{0,4},{4,8},{8,12},{12,14},{14,10},{10,6},{6,2},{2,0},{1,5},{5,9},... | collective-permute-start | bytes 1572872 | tf_op jit(solution)/shard_map/ppermute | solution.py:906
  473.2 29.6 %collective-permute-start.50 = (bf16[256,1024]{1,0:T(8,128)(2,1)S(1)}, bf16[256,1024]{1,0:T(8,128)(2,1)S(1)}, u32[]{:S(2)}, u32[]{:S(2)}) collective-permute-start(bf16[256,1024]{1,0:T(8,128)(2,1)S(1)} %get-tuple-element.237.refs_4_), channel_id=1, source_target_pairs={{0,2},{4,0},{8,4},{12,8},{14,12},{10,14},{6,10},{2,6},{1,3},{5,1},... | collective-permute-start | bytes 1572872 | tf_op jit(solution)/shard_map/ppermute | solution.py:906
  495.7 29.6 %collective-permute-start.54 = (bf16[64,4096]{1,0:T(8,128)(2,1)S(1)}, bf16[64,4096]{1,0:T(8,128)(2,1)S(1)}, u32[]{:S(2)}, u32[]{:S(2)}) collective-permute-start(bf16[64,4096]{1,0:T(8,128)(2,1)S(1)} %ring_own.4.refs_0_), channel_id=1, source_target_pairs={{0,2},{4,0},{8,4},{12,8},{14,12},{10,14},{6,10},{2,6},{1,3},{5,1},... | collective-permute-start | bytes 1572872 | tf_op jit(solution)/shard_map/ppermute | solution.py:906
  500.8 24.4 %collective-permute-start.53 = (bf16[64,4096]{1,0:T(8,128)(2,1)S(1)}, bf16[64,4096]{1,0:T(8,128)(2,1)S(1)}, u32[]{:S(2)}, u32[]{:S(2)}) collective-permute-start(bf16[64,4096]{1,0:T(8,128)(2,1)S(1)} %ring_own.4.refs_0_), channel_id=1, source_target_pairs={{0,4},{4,8},{8,12},{12,14},{14,10},{10,6},{6,2},{2,0},{1,5},{5,9},... | collective-permute-start | bytes 1572872 | tf_op jit(solution)/shard_map/ppermute | solution.py:906
  527.4 34.2 %collective-permute-start.59 = (bf16[64,4096]{1,0:T(8,128)(2,1)S(1)}, bf16[64,4096]{1,0:T(8,128)(2,1)S(1)}, u32[]{:S(2)}, u32[]{:S(2)}) collective-permute-start(bf16[64,4096]{1,0:T(8,128)(2,1)S(1)} %get-tuple-element.260), channel_id=1, source_target_pairs={{0,4},{4,8},{8,12},{12,14},{14,10},{10,6},{6,2},{2,0},{1,5},{5,9},... | collective-permute-start | bytes 1572872 | tf_op jit(solution)/shard_map/ppermute | solution.py:906
  529.1 32.5 %collective-permute-start.60 = (bf16[64,4096]{1,0:T(8,128)(2,1)S(1)}, bf16[64,4096]{1,0:T(8,128)(2,1)S(1)}, u32[]{:S(2)}, u32[]{:S(2)}) collective-permute-start(bf16[64,4096]{1,0:T(8,128)(2,1)S(1)} %get-tuple-element.251.refs_4_), channel_id=1, source_target_pairs={{0,2},{4,0},{8,4},{12,8},{14,12},{10,14},{6,10},{2,6},{1,3},{5,1},... | collective-permute-start | bytes 1572872 | tf_op jit(solution)/shard_map/ppermute | solution.py:906
  559.5 28.9 %collective-permute-start.57 = (bf16[64,4096]{1,0:T(8,128)(2,1)S(1)}, bf16[64,4096]{1,0:T(8,128)(2,1)S(1)}, u32[]{:S(2)}, u32[]{:S(2)}) collective-permute-start(bf16[64,4096]{1,0:T(8,128)(2,1)S(1)} %get-tuple-element.256), channel_id=1, source_target_pairs={{0,4},{4,8},{8,12},{12,14},{14,10},{10,6},{6,2},{2,0},{1,5},{5,9},... | collective-permute-start | bytes 1572872 | tf_op jit(solution)/shard_map/ppermute | solution.py:906
  561.2 29.3 %collective-permute-start.58 = (bf16[64,4096]{1,0:T(8,128)(2,1)S(1)}, bf16[64,4096]{1,0:T(8,128)(2,1)S(1)}, u32[]{:S(2)}, u32[]{:S(2)}) collective-permute-start(bf16[64,4096]{1,0:T(8,128)(2,1)S(1)} %get-tuple-element.257.refs_3_), channel_id=1, source_target_pairs={{0,2},{4,0},{8,4},{12,8},{14,12},{10,14},{6,10},{2,6},{1,3},{5,1},... | collective-permute-start | bytes 1572872 | tf_op jit(solution)/shard_map/ppermute | solution.py:906
  563.7 28.9 %collective-permute-start.67 = (bf16[64,4096]{1,0:T(8,128)(2,1)S(1)}, bf16[64,4096]{1,0:T(8,128)(2,1)S(1)}, u32[]{:S(2)}, u32[]{:S(2)}) collective-permute-start(bf16[64,4096]{1,0:T(8,128)(2,1)S(1)} %get-tuple-element.279), channel_id=1, source_target_pairs={{0,4},{4,8},{8,12},{12,14},{14,10},{10,6},{6,2},{2,0},{1,5},{5,9},... | collective-permute-start | bytes 1572872 | tf_op jit(solution)/shard_map/ppermute | solution.py:906
  565.5 29.1 %collective-permute-start.68 = (bf16[64,4096]{1,0:T(8,128)(2,1)S(1)}, bf16[64,4096]{1,0:T(8,128)(2,1)S(1)}, u32[]{:S(2)}, u32[]{:S(2)}) collective-permute-start(bf16[64,4096]{1,0:T(8,128)(2,1)S(1)} %get-tuple-element.262.refs_4_), channel_id=1, source_target_pairs={{0,2},{4,0},{8,4},{12,8},{14,12},{10,14},{6,10},{2,6},{1,3},{5,1},... | collective-permute-start | bytes 1572872 | tf_op jit(solution)/shard_map/ppermute | solution.py:906
  (116 other events, 1279.4 us)
where the time goes:
time: 620 us; the launch traced here: 610 us
  Pallas kernels  261 us (42%)
  waiting for transfers between devices  185 us (30%)
  starting transfers between devices  126 us (20%)
  local copies, waits for them, and re-layouts  27 us (4%)
  other arithmetic  8.44 us (1%)
    pallas_call x39, Pallas kernels, local_call(): pl.pallas_call(functools.partial(local_kernel, body, near_in, near_out, l...  233 us
    ppermute x48, waiting for transfers between devices, ring_shift(): return lax.ppermute(vals, axis, pairs)  100 us
    all_to_all x11, starting transfers between devices, exchange(): return lax.all_to_all(vals, 'ctx', split_axis=0, concat_axis=0, tiled=True)  54.4 us
    ppermute x48, starting transfers between devices, ring_shift(): return lax.ppermute(vals, axis, pairs)  54.2 us
    ppermute x3, waiting for transfers between devices, butterfly_sum(): got = lax.ppermute(vals, axis, [(i, i ^ by) for i in range(count)])  33.5 us
    pallas_call x15, Pallas kernels, put(): pl.pallas_call(functools.partial(ring_put_kernel, starts, tuple((k % coun...  28.4 us
    all_to_all x11, waiting for transfers between devices, exchange(): return lax.all_to_all(vals, 'ctx', split_axis=0, concat_axis=0, tiled=True)  23.7 us
    unnamed x119, local copies, waits for them, and re-layouts  22.7 us
  transfers between devices with their start and end apart: 84, of which 40 were waited for; matrix products, arithmetic and copies ran while one was open for 3% of the time, Pallas kernels for 39%

commit v1 on v0

--- a/solution.py
+++ b/solution.py
@@ -13,9 +13,9 @@
 ROPE_BASE = 10000.0
 MASKED_SCORE = -1e30
 LANES = 128
-VMEM_LIMIT = 56 * 1024 * 1024
-TAIL_LIMIT = 56 * 1024 * 1024
-RING_LIMIT = 50 * 1024 * 1024
+VMEM_LIMIT = 50 * 1024 * 1024
+TAIL_LIMIT = VMEM_LIMIT
+RING_LIMIT = VMEM_LIMIT
 INV_SQRT2 = 0.7071067811865476
 INV_SQRT_2PI = 0.3989422804014327
 
@@ -236,10 +236,10 @@
         functools.partial(qkv_kernel, got is None),
         "qkv_proj",
         [wsh],
-        [given, vecs, qkv_b, tab] if got is None else [far(given), vecs, qkv_b, tab, got],
+        [given, vecs, qkv_b, tab] if got is None else [given, vecs, qkv_b, tab, got],
         [w_own, w_oth],
-        [far(shape_of((pairs, 3, rows, LANES), bf16)), far(shape_of((rows, dim), bf16))]
-        + [far(shape_of((2, rows, half), bf16))] * 2,
+        [shape_of((pairs, 3, rows, LANES), bf16), shape_of((rows, dim), bf16)]
+        + [shape_of((2, rows, half), bf16)] * 2,
         [pltpu.VMEM((3, 2, half, dim), bf16), pltpu.SemaphoreType.DMA((3, 2))],
     )
 
@@ -306,15 +306,15 @@
     rows, half = own.shape[1:]
     dim = dn_own.shape[1]
     ff = up_own.shape[1]
-    out_shape = [far(shape_of((rows, dim), f32))]
+    out_shape = [shape_of((rows, dim), f32)]
     if save:
-        out_shape += [far(shape_of((ff, rows), bf16))]
-        out_shape += [far(shape_of((ff // 2, rows), bf16))] * 2
+        out_shape += [shape_of((ff, rows), bf16)]
+        out_shape += [shape_of((ff // 2, rows), bf16)] * 2
     return local_call(
         functools.partial(mlp_kernel, save),
         "mlp_forward",
         [wsh],
-        [far(own), far(oth), up_b, down_b],
+        [own, oth, up_b, down_b],
         [up_own, up_oth, dn_own, dn_oth],
         out_shape,
         ff_scratch(half, ff, dim),
@@ -346,9 +346,9 @@
         mlp_back_kernel,
         "mlp_backward",
         [wsh],
-        [far(dy), far(slope)],
+        [dy, slope],
         [up_own, up_oth, dn_own, dn_oth],
-        [far(shape_of(slope.shape, bf16)), far(shape_of((rows, dim), f32))],
+        [shape_of(slope.shape, bf16), shape_of((rows, dim), f32)],
         [pltpu.VMEM((half, rows), f32), pltpu.VMEM((half, rows), f32)] + ff_scratch(half, ff, dim),
         after,
         limit,
@@ -440,7 +440,7 @@
         [loc],
         [qkv],
         [],
-        [far(shape_of((count, rows, LANES), bf16)), far(shape_of((2, seq), f32))],
+        [shape_of((count, rows, LANES), bf16), shape_of((2, seq), f32)],
         [
             pltpu.VMEM((seq, LANES), bf16),
             pltpu.VMEM((seq, LANES), bf16),
@@ -508,9 +508,9 @@
         functools.partial(attend_back_kernel, 256, part),
         "attention_backward",
         [loc],
-        [da, far(qkv), far(lse)],
+        [da, qkv, lse],
         [],
-        [far(shape_of(qkv.shape, bf16))],
+        [shape_of(qkv.shape, bf16)],
         [pltpu.VMEM((seq, LANES), bf16)] * 4
         + [pltpu.VMEM((LANES, seq), bf16), pltpu.VMEM((seq, LANES), bf16)]
         + [pltpu.VMEM((seq, LANES), f32)] * 2,
@@ -645,9 +645,9 @@
         functools.partial(proj_kernel, 1 if a.ndim == 4 else None),
         "attn_out",
         [wsh],
-        [a, bias, far(x), far(mlp)],
+        [a, bias, x, mlp],
         [p_own, p_oth],
-        [far(shape_of((rows, dim), bf16))] + [far(shape_of((rows, half), bf16))] * 2,
+        [shape_of((rows, dim), bf16)] + [shape_of((rows, half), bf16)] * 2,
         half_scratch(p_own),
         after,
         limit,
@@ -681,8 +681,8 @@
 def da_call(given, got, p_own, p_oth, wsh, joined=None):
     rows, dim = given.shape
     pairs = dim // LANES
-    arrays = [far(given)] + ([] if got is None else [got])
-    arrays += [] if joined is None else [far(joined)]
+    arrays = [given] + ([] if got is None else [got])
+    arrays += [] if joined is None else [joined]
     shape = (pairs, rows, LANES) if joined is None else (pairs, 2, rows, LANES)
     return local_call(
         functools.partial(da_kernel, got is None),
@@ -690,7 +690,7 @@
         [wsh],
         arrays,
         [p_own, p_oth],
-        [far(shape_of(shape, bf16)), far(shape_of((rows, dim), bf16))],
+        [shape_of(shape, bf16), shape_of((rows, dim), bf16)],
         half_scratch(p_own),
     )
 
@@ -737,9 +737,9 @@
         dx_kernel,
         "section_input_grad",
         [wsh],
-        [dqkv, tab, vecs, far(x), far(dy), far(dnm)],
+        [dqkv, tab, vecs, x, dy, dnm],
         [w_own, w_oth],
-        [far(shape_of(o, t)) for o, t in ((dqkv.shape, bf16), ((rows, dim), bf16), ((4, dim), f32))],
+        [shape_of(o, t) for o, t in ((dqkv.shape, bf16), ((rows, dim), bf16), ((4, dim), f32))],
         [pltpu.VMEM((rows, 3 * dim), bf16)] + half_scratch(w_own),
         after,
         limit,
@@ -1041,7 +1041,7 @@
             [idx],
             [ahead, behind],
             [own],
-            [far(chunk), far(chunk)],
+            [chunk, chunk],
             taken(2),
             [token],
             RING_LIMIT,
@@ -1055,7 +1055,7 @@
         [idx],
         [ahead, behind],
         [own],
-        [far(chunk)],
+        [chunk],
         taken(1),
         [token],
         RING_LIMIT,
@@ -1073,19 +1073,23 @@
     yield [total.reshape(full_rows, -1) for total in totals]
 
 
+def add_kernel(inputs, weights, outputs):
+    outputs[0].ref[...] = inputs[0].ref()[...] + inputs[1].ref()[...]
+
+
 def butterfly_sum(vals, axis):
     count = lax.axis_size(axis)
     by = 1
     token = yield None
     if count & (count - 1):
-        yield lax.psum(tied(token, vals)[0], axis)
+        yield lax.psum(vals, axis)
         return
-    (vals,) = tied(token, vals)
     while by < count:
         got = lax.ppermute(vals, axis, [(i, i ^ by) for i in range(count)])
         token = yield None
-        (got,) = tied(token, got)
-        vals = vals + got
+        (vals,) = local_call(
+            add_kernel, "small_add", [], [vals, got], [], [shape_of(vals.shape, f32)], [], [token]
+        )
         by *= 2
     yield vals
 
@@ -1250,7 +1254,8 @@
     qkv_2 = moved(tied(da_a, made_b[0])[0])
     norms_b = swap(made_b[3])
     mlp_b = mlp(made_b, True)
-    att_b, kept_b = attend(qkv_2, [mlp_b[0], norms_b])
+    _, dnm_a = mlp_back(dy_a, mlp_b)
+    att_b, kept_b = attend(qkv_2, [dnm_a, norms_b])
     att_b = moved(att_b)
     gt_b = swap(mlp_b[3])
     dqkv_a_ = attend_back(kept_b, da_a, [gt_b])
@@ -1261,7 +1266,6 @@
     qkv_3 = moved(tied(dqkv_a, made_c[0])[0])
     norms_c = swap(made_c[3])
     a_b_oth = swap(a_b[1])
-    _, dnm_a = mlp_back(dy_a, mlp_b, [made_c[1]])
     _, dx_a, _ = input_grad_of(dqkv_a, made_b, dy_a, dnm_a, [norms_c, a_b_oth])
     got_a = pass_on(dx_a, -1)
     mlp_c = mlp_call(
@@ -1355,7 +1359,7 @@
     summed = None
     while any(left.values()):
         token = turn((up_ring, attn_ring, down_ring, attn_ring)[at % 4], token)
-        if at % 2 == 0 and summed is None:
+        if at % 4 == 0 and summed is None:
             summed = small_ring.send(token)
         at += 1
     while summed is None:

time: 620 us -> 618 us (level)
  Pallas kernels: 261 us -> 215 us
  local copies, waits for them, and re-layouts: 27 us -> 69.5 us
    pallas_call x39 -> x42, Pallas kernels: 233 us -> 185 us  [local_call(): pl.pallas_call(functools.partial(local_kernel, body, near_in, near_out, l...]
    unnamed x119 -> x239, local copies, waits for them, and re-layouts: 22.7 us -> 64.3 us
  transfers between devices with their start and end apart: 84 -> 84, of which waited for: 40 -> 40; matrix products, arithmetic and copies ran while one was open for 3% -> 2% of each run, Pallas kernels for 39% -> 32%
where the time goes in v1:
time: 618 us; the launch traced here: 606 us
  Pallas kernels  215 us (35%)
  waiting for transfers between devices  188 us (30%)
  starting transfers between devices  127 us (21%)
  local copies, waits for them, and re-layouts  69.5 us (11%)
    pallas_call x42, Pallas kernels, local_call(): pl.pallas_call(functools.partial(local_kernel, body, near_in, near_out, l...  185 us
    ppermute x48, waiting for transfers between devices, ring_shift(): return lax.ppermute(vals, axis, pairs)  99.6 us
    unnamed x239, local copies, waits for them, and re-layouts  64.3 us
    all_to_all x11, starting transfers between devices, exchange(): return lax.all_to_all(vals, 'ctx', split_axis=0, concat_axis=0, tiled=True)  56.8 us
    ppermute x48, starting transfers between devices, ring_shift(): return lax.ppermute(vals, axis, pairs)  55.7 us
    ppermute x3, waiting for transfers between devices, butterfly_sum(): got = lax.ppermute(vals, axis, [(i, i ^ by) for i in range(count)])  37 us
    pallas_call x15, Pallas kernels, put(): pl.pallas_call(functools.partial(ring_put_kernel, starts, tuple((k % coun...  30.1 us
    all_to_all x11, waiting for transfers between devices, exchange(): return lax.all_to_all(vals, 'ctx', split_axis=0, concat_axis=0, tiled=True)  21.9 us
  transfers between devices with their start and end apart: 84, of which 40 were waited for; matrix products, arithmetic and copies ran while one was open for 2% of the time, Pallas kernels for 32%

profile of v1, /device:TPU:0, one launch (start us, length us, event | category | flops | bytes accessed | tf_op | source)
XLA Modules:
  0.0 606.5 jit_solution(1743906519905018626)
XLA Ops:
  15.4 7.2 %all-to-all-start = ((bf16[8,3,128,128]{3,2,1,0:T(8,128)(2,1)}), bf16[8,3,128,128]{3,2,1,0:T(8,128)(2,1)}, u32[]{:S(2)}, u32[]{:S(2)}) async-start(bf16[8,3,128,128]{3,2,1,0:T(8,128)(2,1)} %get-tuple-element.148), calls=%async_computation | async-start | bytes 1572864 | tf_op jit(solution)/shard_map/all_to_all | solution.py:1206
  24.8 7.6 %mlp_forward.3.refs_2_.refs_4_ = f32[128,1024]{1,0:T(8,128)S(1)} custom-call(s32[2]{0:T(128)S(1)} %pad_add_fusion.refs_0_, bf16[2,128,512]{2,1,0:T(8,128)(2,1)S(1)} %copy-done.87, bf16[2,128,512]{2,1,0:T(8,128)(2,1)S(1)} %copy-done.89, f32[1,4096]{1,0:T(1,128)S(1)} %bitcast.60, f32[1,1024]{1,0:T(1,128)S(1)} %get-tuple-element.320.refs_4_, ...), custom_call_target="tpu_custom_call" | custom-call | flops 1 | bytes 1 | tf_op jit(solution)/shard_map/mlp_forward/pallas_call | solution.py:210
  33.3 9.9 %all-to-all-done.refs_1_ = bf16[8,3,128,128]{3,2,1,0:T(8,128)(2,1)} async-done(((bf16[8,3,128,128]{3,2,1,0:T(8,128)(2,1)}), bf16[8,3,128,128]{3,2,1,0:T(8,128)(2,1)}, u32[]{:S(2)}, u32[]{:S(2)}) %all-to-all-start) | async-done | bytes 786464 | tf_op jit(solution)/shard_map/all_to_all | solution.py:1206
  95.2 8.5 %mlp_forward.4 = (f32[128,1024]{1,0:T(8,128)S(1)}, bf16[4096,128]{1,0:T(8,128)(2,1)S(1)}, bf16[2048,128]{1,0:T(8,128)(2,1)S(1)}, bf16[2048,128]{1,0:T(8,128)(2,1)}) custom-call(s32[2]{0:T(128)S(1)} %pad_add_fusion.refs_0_, bf16[2,128,512]{2,1,0:T(8,128)(2,1)S(1)} %copy-done.16, bf16[2,128,512]{2,1,0:T(8,128)(2,1)S(1)} %copy-done.91, f32[1,4096]{1,0:T(1,128)S(1)} %bitcast.61, ...), custom_call_target="tpu_custom_call" | custom-call | flops 1 | bytes 1 | tf_op jit(solution)/shard_map/mlp_forward/pallas_call | solution.py:210
  105.7 10.3 %mlp_backward.3 = (bf16[4096,128]{1,0:T(8,128)(2,1)}, f32[128,1024]{1,0:T(8,128)S(1)}) custom-call(s32[2]{0:T(128)S(1)} %pad_add_fusion.refs_0_, bf16[128,1024]{1,0:T(8,128)(2,1)S(1)} %copy-done.43, bf16[4096,128]{1,0:T(8,128)(2,1)S(1)} %get-tuple-element.164.refs_2_, bf16[512,4096]{1,0:T(8,128)(2,1)} %bitcast.69, ...), custom_call_target="tpu_custom_call" | custom-call | flops 1 | bytes 1 | tf_op jit(solution)/shard_map/mlp_backward/pallas_call | solution.py:210
  124.6 6.5 %all-to-all-start.5 = ((bf16[8,128,128]{2,1,0:T(8,128)(2,1)}), bf16[8,128,128]{2,1,0:T(8,128)(2,1)}, u32[]{:S(2)}, u32[]{:S(2)}) async-start(bf16[8,128,128]{2,1,0:T(8,128)(2,1)} %get-tuple-element.168), calls=%async_computation.5 | async-start | bytes 524288 | tf_op jit(solution)/shard_map/all_to_all | solution.py:1206
  131.1 7.5 %attention_backward.3.refs_7_ = bf16[8,3,128,128]{3,2,1,0:T(8,128)(2,1)} custom-call(s32[16]{0:T(128)S(1)} %add_reduce_fusion.refs_0_, bf16[8,128,128]{2,1,0:T(8,128)(2,1)} %all-to-all-done.2.refs_1_, bf16[8,3,128,128]{3,2,1,0:T(8,128)(2,1)S(1)} %all-to-all-done.3.refs_1_.refs_2_, f32[2,1024]{1,0:T(2,128)S(1)} %get-tuple-element.166.refs_3_, ...), custom_call_target="tpu_custom_call" | custom-call | flops 1 | bytes 1 | tf_op jit(solution)/shard_map/attention_backward/pallas_call | solution.py:210
  177.9 6.5 %section_input_grad.3 = (bf16[8,3,128,128]{3,2,1,0:T(8,128)(2,1)}, bf16[128,1024]{1,0:T(8,128)(2,1)S(1)}, f32[4,1024]{1,0:T(4,128)}) custom-call(s32[2]{0:T(128)S(1)} %pad_add_fusion.refs_0_, bf16[8,3,128,128]{3,2,1,0:T(8,128)(2,1)} %all-to-all-done.4.refs_1_, f32[3,128,128]{2,1,0:T(8,128)S(1)} %pad_maximum_fusion.refs_4_.refs_2_, ...), custom_call_target="tpu_custom_call" | custom-call | flops 1 | bytes 1 | tf_op jit(solution)/shard_map/section_input_grad/pallas_call | solution.py:210
  185.9 8.5 %mlp_forward.5 = (f32[128,1024]{1,0:T(8,128)S(1)}, bf16[4096,128]{1,0:T(8,128)(2,1)S(1)}, bf16[2048,128]{1,0:T(8,128)(2,1)S(1)}, bf16[2048,128]{1,0:T(8,128)(2,1)}) custom-call(s32[2]{0:T(128)S(1)} %pad_add_fusion.refs_0_, bf16[2,128,512]{2,1,0:T(8,128)(2,1)S(1)} %copy-done.20, bf16[2,128,512]{2,1,0:T(8,128)(2,1)S(1)} %copy-done.85, f32[1,4096]{1,0:T(1,128)S(1)} %bitcast.62, ...), custom_call_target="tpu_custom_call" | custom-call | flops 1 | bytes 1 | tf_op jit(solution)/shard_map/mlp_forward/pallas_call | solution.py:210
  199.6 5.9 all-to-all-start.7
  216.0 6.8 %attention_backward.4.refs_7_ = bf16[8,3,128,128]{3,2,1,0:T(8,128)(2,1)S(1)} custom-call(s32[16]{0:T(128)S(1)} %add_reduce_fusion.refs_0_, bf16[8,128,128]{2,1,0:T(8,128)(2,1)} %all-to-all-done.7.refs_1_, bf16[8,3,128,128]{3,2,1,0:T(8,128)(2,1)} %all-to-all-done.6.refs_1_.refs_2_, f32[2,1024]{1,0:T(2,128)S(1)} %get-tuple-element.184.refs_3_, ...), custom_call_target="tpu_custom_call" | custom-call | flops 1 | bytes 1 | tf_op jit(solution)/shard_map/attention_backward/pallas_call | solution.py:210
  230.6 10.0 %mlp_backward.4 = (bf16[4096,128]{1,0:T(8,128)(2,1)S(1)}, f32[128,1024]{1,0:T(8,128)S(1)}) custom-call(s32[2]{0:T(128)S(1)} %pad_add_fusion.refs_0_, bf16[128,1024]{1,0:T(8,128)(2,1)S(1)} %get-tuple-element.183.refs_2_.refs_1_.refs_5_.refs_6_.refs_14_, bf16[4096,128]{1,0:T(8,128)(2,1)S(1)} %copy-done.64, bf16[512,4096]{1,0:T(8,128)(2,1)} %bitcast.71, ...), custom_call_target="tpu_custom_call" | custom-call | flops 1 | bytes 1 | tf_op jit(solution)/shard_map/mlp_backward/pallas_call | solution.py:210
  257.2 9.7 %collective-permute-done.16.refs_2_ = bf16[128,1024]{1,0:T(8,128)(2,1)S(1)} collective-permute-done((bf16[128,1024]{1,0:T(8,128)(2,1)S(1)}, bf16[128,1024]{1,0:T(8,128)(2,1)S(1)}, u32[]{:S(2)}, u32[]{:S(2)}) %collective-permute-start.16) | collective-permute-done | bytes 262176 | tf_op jit(solution)/shard_map/ppermute | solution.py:1103
  288.1 6.4 %collective-permute-done.18.refs_1_ = bf16[256,512]{1,0:T(8,128)(2,1)S(1)} collective-permute-done((bf16[256,512]{1,0:T(8,128)(2,1)S(1)}, bf16[256,512]{1,0:T(8,128)(2,1)S(1)}, u32[]{:S(2)}, u32[]{:S(2)}) %collective-permute-start.18) | collective-permute-done | bytes 262176 | tf_op jit(solution)/shard_map/ppermute | solution.py:906
  301.2 10.3 %mlp_backward.5 = (bf16[4096,128]{1,0:T(8,128)(2,1)}, f32[128,1024]{1,0:T(8,128)S(1)}) custom-call(s32[2]{0:T(128)S(1)} %pad_add_fusion.refs_0_, bf16[128,1024]{1,0:T(8,128)(2,1)S(1)} %copy-done.11, bf16[4096,128]{1,0:T(8,128)(2,1)S(1)} %copy-done.14, bf16[512,4096]{1,0:T(8,128)(2,1)} %bitcast.72, bf16[512,4096]{1,0:T(8,128)(2,1)} %collective-permute-done.2.refs_6_.refs_4_, ...), custom_call_target="tpu_custom_call" | custom-call | flops 1 | bytes 1 | tf_op jit(solution)/shard_map/mlp_backward/pallas_call | solution.py:210
  313.4 6.6 %attention_backward.5.refs_4_ = bf16[8,3,128,128]{3,2,1,0:T(8,128)(2,1)S(1)} custom-call(s32[16]{0:T(128)S(1)} %add_reduce_fusion.refs_0_, bf16[8,2,128,128]{3,2,1,0:T(8,128)(2,1)} %all-to-all-done.9.refs_1_, bf16[8,3,128,128]{3,2,1,0:T(8,128)(2,1)S(1)} %all-to-all-done.3.refs_1_.refs_2_, f32[2,1024]{1,0:T(2,128)S(1)} %get-tuple-element.166.refs_3_, ...), custom_call_target="tpu_custom_call" | custom-call | flops 1 | bytes 1 | tf_op jit(solution)/shard_map/attention_backward/pallas_call | solution.py:210
  335.3 7.4 %up_grad.1 = (bf16[512,4096]{1,0:T(8,128)(2,1)}, bf16[64,2048]{1,0:T(8,128)(2,1)S(1)}, bf16[64,2048]{1,0:T(8,128)(2,1)S(1)}, f32[1,4096]{1,0:T(1,128)S(1)}) custom-call(s32[8]{0:T(128)S(1)} %and_select_fusion.refs_0_.idx_ref, bf16[2,128,512]{2,1,0:T(8,128)(2,1)S(1)} %copy-done.17, bf16[2,128,512]{2,1,0:T(8,128)(2,1)S(1)} %copy-done.21, ...), custom_call_target="tpu_custom_call" | custom-call | flops 1 | bytes 1 | tf_op jit(solution)/shard_map/up_grad/pallas_call | solution.py:210
  342.8 8.1 %collective-permute-done.22.refs_1_ = bf16[256,1024]{1,0:T(8,128)(2,1)S(1)} collective-permute-done((bf16[256,1024]{1,0:T(8,128)(2,1)S(1)}, bf16[256,1024]{1,0:T(8,128)(2,1)S(1)}, u32[]{:S(2)}, u32[]{:S(2)}) %collective-permute-start.22) | collective-permute-done | bytes 524320 | tf_op jit(solution)/shard_map/ppermute | solution.py:906
  363.0 14.6 %collective-permute-done.27.refs_1_ = bf16[64,2048]{1,0:T(8,128)(2,1)S(1)} collective-permute-done((bf16[64,2048]{1,0:T(8,128)(2,1)S(1)}, bf16[64,2048]{1,0:T(8,128)(2,1)S(1)}, u32[]{:S(2)}, u32[]{:S(2)}) %collective-permute-start.27) | collective-permute-done | bytes 262176 | tf_op jit(solution)/shard_map/ppermute | solution.py:906
  414.5 7.2 %attn_grad.1 = (bf16[512,4096]{1,0:T(8,128)(2,1)}, bf16[64,2048]{1,0:T(8,128)(2,1)S(1)}, bf16[64,2048]{1,0:T(8,128)(2,1)S(1)}, f32[1,4096]{1,0:T(1,128)S(1)}) custom-call(s32[8]{0:T(128)S(1)} %and_select_fusion.refs_0_.idx_ref, bf16[2,128,512]{2,1,0:T(8,128)(2,1)S(1)} %copy-done.18, bf16[2,128,512]{2,1,0:T(8,128)(2,1)S(1)} %copy-done.22, ...), custom_call_target="tpu_custom_call" | custom-call | flops 1 | bytes 1 | tf_op jit(solution)/shard_map/attn_grad/pallas_call | solution.py:210
  446.3 7.1 %collective-permute-done.39.refs_1_ = bf16[64,4096]{1,0:T(8,128)(2,1)S(1)} collective-permute-done((bf16[64,4096]{1,0:T(8,128)(2,1)S(1)}, bf16[64,4096]{1,0:T(8,128)(2,1)S(1)}, u32[]{:S(2)}, u32[]{:S(2)}) %collective-permute-start.39) | collective-permute-done | bytes 524320 | tf_op jit(solution)/shard_map/ppermute | solution.py:906
  491.8 6.6 %collective-permute-done.47.refs_1_ = bf16[64,4096]{1,0:T(8,128)(2,1)S(1)} collective-permute-done((bf16[64,4096]{1,0:T(8,128)(2,1)S(1)}, bf16[64,4096]{1,0:T(8,128)(2,1)S(1)}, u32[]{:S(2)}, u32[]{:S(2)}) %collective-permute-start.47) | collective-permute-done | bytes 524320 | tf_op jit(solution)/shard_map/ppermute | solution.py:906
  531.8 20.8 %collective-permute-done.64.refs_1_ = f32[12,512]{1,0:T(8,128)S(1)} collective-permute-done((f32[12,512]{1,0:T(8,128)S(1)}, f32[12,512]{1,0:T(8,128)S(1)}, u32[]{:S(2)}, u32[]{:S(2)}) %collective-permute-start.64) | collective-permute-done | bytes 24608 | tf_op jit(solution)/shard_map/ppermute | solution.py:1088
  570.3 16.2 %collective-permute-done.66.refs_1_ = f32[12,512]{1,0:T(8,128)S(1)} collective-permute-done((f32[12,512]{1,0:T(8,128)S(1)}, f32[12,512]{1,0:T(8,128)S(1)}, u32[]{:S(2)}, u32[]{:S(2)}) %collective-permute-start.66) | collective-permute-done | bytes 24608 | tf_op jit(solution)/shard_map/ppermute | solution.py:1088
  (486 shorter events, 387.8 us)
Async XLA Ops:
  15.4 27.8 %all-to-all-start = ((bf16[8,3,128,128]{3,2,1,0:T(8,128)(2,1)}), bf16[8,3,128,128]{3,2,1,0:T(8,128)(2,1)}, u32[]{:S(2)}, u32[]{:S(2)}) async-start(bf16[8,3,128,128]{3,2,1,0:T(8,128)(2,1)} %get-tuple-element.148), calls=%async_computation | async-start | bytes 1572864 | tf_op jit(solution)/shard_map/all_to_all | solution.py:1206
  22.6 33.1 %collective-permute-start.4 = (bf16[512,1024]{1,0:T(8,128)(2,1)S(1)}, bf16[512,1024]{1,0:T(8,128)(2,1)S(1)}, u32[]{:S(2)}, u32[]{:S(2)}) collective-permute-start(bf16[512,1024]{1,0:T(8,128)(2,1)S(1)} %bitcast.53), channel_id=1, source_target_pairs={{0,1},{1,0},{2,3},{3,2},{4,5},{5,4},{6,7},{7,6},{8,9},{9,8},{10,11... | collective-permute-start | bytes 3145736 | tf_op jit(solution)/shard_map/ppermute | solution.py:1098
  87.5 30.0 %all-to-all-start.3 = ((bf16[8,3,128,128]{3,2,1,0:T(8,128)(2,1)}), bf16[8,3,128,128]{3,2,1,0:T(8,128)(2,1)S(1)}, u32[]{:S(2)}, u32[]{:S(2)}) async-start(bf16[8,3,128,128]{3,2,1,0:T(8,128)(2,1)} %get-tuple-element.161), calls=%async_computation.3 | async-start | bytes 1572864 | tf_op jit(solution)/shard_map/all_to_all | solution.py:1206
  105.2 25.9 %collective-permute-start.7 = (bf16[2048,128]{1,0:T(8,128)(2,1)}, bf16[2048,128]{1,0:T(8,128)(2,1)}, u32[]{:S(2)}, u32[]{:S(2)}) collective-permute-start(bf16[2048,128]{1,0:T(8,128)(2,1)} %get-tuple-element.167), channel_id=1, source_target_pairs={{0,1},{1,0},{2,3},{3,2},{4,5},{5,4},{6,7},{7,6},{8,9},{9,8},{10,11... | collective-permute-start | bytes 1572872 | tf_op jit(solution)/shard_map/ppermute | solution.py:1098
  140.2 27.0 %all-to-all-start.4 = ((bf16[8,3,128,128]{3,2,1,0:T(8,128)(2,1)}), bf16[8,3,128,128]{3,2,1,0:T(8,128)(2,1)}, u32[]{:S(2)}, u32[]{:S(2)}) async-start(bf16[8,3,128,128]{3,2,1,0:T(8,128)(2,1)} %attention_backward.3.refs_7_), calls=%async_computation.4 | async-start | bytes 1572864 | tf_op jit(solution)/shard_map/all_to_all | solution.py:1206
  167.2 32.4 %all-to-all-start.6 = ((bf16[8,3,128,128]{3,2,1,0:T(8,128)(2,1)}), bf16[8,3,128,128]{3,2,1,0:T(8,128)(2,1)}, u32[]{:S(2)}, u32[]{:S(2)}) async-start(bf16[8,3,128,128]{3,2,1,0:T(8,128)(2,1)} %get-tuple-element.173), calls=%async_computation.6 | async-start | bytes 1572864 | tf_op jit(solution)/shard_map/all_to_all | solution.py:1206
  223.7 24.2 %all-to-all-start.8 = ((bf16[8,3,128,128]{3,2,1,0:T(8,128)(2,1)}), bf16[8,3,128,128]{3,2,1,0:T(8,128)(2,1)}, u32[]{:S(2)}, u32[]{:S(2)}) async-start(bf16[8,3,128,128]{3,2,1,0:T(8,128)(2,1)} %copy-done.3), calls=%async_computation.8 | async-start | bytes 1572864 | tf_op jit(solution)/shard_map/all_to_all | solution.py:1206
  270.3 42.0 %all-to-all-start.9 = ((bf16[8,2,128,128]{3,2,1,0:T(8,128)(2,1)}), bf16[8,2,128,128]{3,2,1,0:T(8,128)(2,1)}, u32[]{:S(2)}, u32[]{:S(2)}) async-start(bf16[8,2,128,128]{3,2,1,0:T(8,128)(2,1)} %copy-done.77), calls=%async_computation.9 | async-start | bytes 1048576 | tf_op jit(solution)/shard_map/all_to_all | solution.py:1206
  298.8 26.7 %collective-permute-start.20 = (bf16[256,1024]{1,0:T(8,128)(2,1)}, bf16[256,1024]{1,0:T(8,128)(2,1)}, u32[]{:S(2)}, u32[]{:S(2)}) collective-permute-start(bf16[256,1024]{1,0:T(8,128)(2,1)} %get-tuple-element.201), channel_id=1, source_target_pairs={{0,4},{4,8},{8,12},{12,14},{14,10},{10,6},{6,2},{2,0},{1,5},{5,9},... | collective-permute-start | bytes 1572872 | tf_op jit(solution)/shard_map/ppermute | solution.py:906
  300.3 25.2 %collective-permute-start.21 = (bf16[256,1024]{1,0:T(8,128)(2,1)}, bf16[256,1024]{1,0:T(8,128)(2,1)}, u32[]{:S(2)}, u32[]{:S(2)}) collective-permute-start(bf16[256,1024]{1,0:T(8,128)(2,1)} %get-tuple-element.202.refs_7_), channel_id=1, source_target_pairs={{0,2},{4,0},{8,4},{12,8},{14,12},{10,14},{6,10},{2,6},{1,3},{5,1},... | collective-permute-start | bytes 1572872 | tf_op jit(solution)/shard_map/ppermute | solution.py:906
  320.9 63.7 %all-to-all-start.10 = ((bf16[8,3,128,128]{3,2,1,0:T(8,128)(2,1)}), bf16[8,3,128,128]{3,2,1,0:T(8,128)(2,1)}, u32[]{:S(2)}, u32[]{:S(2)}) async-start(bf16[8,3,128,128]{3,2,1,0:T(8,128)(2,1)} %copy-done.5), calls=%async_computation.10 | async-start | bytes 1572864 | tf_op jit(solution)/shard_map/all_to_all | solution.py:1206
  355.2 38.4 %collective-permute-start.25 = (bf16[256,1024]{1,0:T(8,128)(2,1)}, bf16[256,1024]{1,0:T(8,128)(2,1)}, u32[]{:S(2)}, u32[]{:S(2)}) collective-permute-start(bf16[256,1024]{1,0:T(8,128)(2,1)} %get-tuple-element.208), channel_id=1, source_target_pairs={{0,4},{4,8},{8,12},{12,14},{14,10},{10,6},{6,2},{2,0},{1,5},{5,9},... | collective-permute-start | bytes 1572872 | tf_op jit(solution)/shard_map/ppermute | solution.py:906
  361.0 32.6 %collective-permute-start.26 = (bf16[256,1024]{1,0:T(8,128)(2,1)}, bf16[256,1024]{1,0:T(8,128)(2,1)}, u32[]{:S(2)}, u32[]{:S(2)}) collective-permute-start(bf16[256,1024]{1,0:T(8,128)(2,1)} %get-tuple-element.209.refs_4_), channel_id=1, source_target_pairs={{0,2},{4,0},{8,4},{12,8},{14,12},{10,14},{6,10},{2,6},{1,3},{5,1},... | collective-permute-start | bytes 1572872 | tf_op jit(solution)/shard_map/ppermute | solution.py:906
  436.7 29.7 %collective-permute-start.46 = (bf16[64,4096]{1,0:T(8,128)(2,1)S(1)}, bf16[64,4096]{1,0:T(8,128)(2,1)S(1)}, u32[]{:S(2)}, u32[]{:S(2)}) collective-permute-start(bf16[64,4096]{1,0:T(8,128)(2,1)S(1)} %get-tuple-element.228.refs_4_), channel_id=1, source_target_pairs={{0,2},{4,0},{8,4},{12,8},{14,12},{10,14},{6,10},{2,6},{1,3},{5,1},... | collective-permute-start | bytes 1572872 | tf_op jit(solution)/shard_map/ppermute | solution.py:906
  459.2 29.7 %collective-permute-start.50 = (bf16[256,1024]{1,0:T(8,128)(2,1)S(1)}, bf16[256,1024]{1,0:T(8,128)(2,1)S(1)}, u32[]{:S(2)}, u32[]{:S(2)}) collective-permute-start(bf16[256,1024]{1,0:T(8,128)(2,1)S(1)} %get-tuple-element.233.refs_4_), channel_id=1, source_target_pairs={{0,2},{4,0},{8,4},{12,8},{14,12},{10,14},{6,10},{2,6},{1,3},{5,1},... | collective-permute-start | bytes 1572872 | tf_op jit(solution)/shard_map/ppermute | solution.py:906
  481.7 29.7 %collective-permute-start.54 = (bf16[64,4096]{1,0:T(8,128)(2,1)S(1)}, bf16[64,4096]{1,0:T(8,128)(2,1)S(1)}, u32[]{:S(2)}, u32[]{:S(2)}) collective-permute-start(bf16[64,4096]{1,0:T(8,128)(2,1)S(1)} %ring_own.4.refs_0_), channel_id=1, source_target_pairs={{0,2},{4,0},{8,4},{12,8},{14,12},{10,14},{6,10},{2,6},{1,3},{5,1},... | collective-permute-start | bytes 1572872 | tf_op jit(solution)/shard_map/ppermute | solution.py:906
  487.1 25.1 %collective-permute-start.53 = (bf16[64,4096]{1,0:T(8,128)(2,1)S(1)}, bf16[64,4096]{1,0:T(8,128)(2,1)}, u32[]{:S(2)}, u32[]{:S(2)}) collective-permute-start(bf16[64,4096]{1,0:T(8,128)(2,1)S(1)} %ring_own.4.refs_0_), channel_id=1, source_target_pairs={{0,4},{4,8},{8,12},{12,14},{14,10},{10,6},{6,2},{2,0},{1,5},{5,9},... | collective-permute-start | bytes 1572872 | tf_op jit(solution)/shard_map/ppermute | solution.py:906
  525.7 26.9 %collective-permute-start.55 = (bf16[64,4096]{1,0:T(8,128)(2,1)S(1)}, bf16[64,4096]{1,0:T(8,128)(2,1)S(1)}, u32[]{:S(2)}, u32[]{:S(2)}) collective-permute-start(bf16[64,4096]{1,0:T(8,128)(2,1)S(1)} %get-tuple-element.248), channel_id=1, source_target_pairs={{0,4},{4,8},{8,12},{12,14},{14,10},{10,6},{6,2},{2,0},{1,5},{5,9},... | collective-permute-start | bytes 1572872 | tf_op jit(solution)/shard_map/ppermute | solution.py:906
  527.4 33.2 %collective-permute-start.60 = (bf16[64,4096]{1,0:T(8,128)(2,1)S(1)}, bf16[64,4096]{1,0:T(8,128)(2,1)S(1)}, u32[]{:S(2)}, u32[]{:S(2)}) collective-permute-start(bf16[64,4096]{1,0:T(8,128)(2,1)S(1)} %get-tuple-element.247.refs_4_.refs_2_), channel_id=1, source_target_pairs={{0,2},{4,0},{8,4},{12,8},{14,12},{10,14},{6,10},{2,6},{1,3},{5,1},... | collective-permute-start | bytes 1572872 | tf_op jit(solution)/shard_map/ppermute | solution.py:906
  529.1 31.4 %collective-permute-start.59 = (bf16[64,4096]{1,0:T(8,128)(2,1)}, bf16[64,4096]{1,0:T(8,128)(2,1)S(1)}, u32[]{:S(2)}, u32[]{:S(2)}) collective-permute-start(bf16[64,4096]{1,0:T(8,128)(2,1)} %copy-done.108), channel_id=1, source_target_pairs={{0,4},{4,8},{8,12},{12,14},{14,10},{10,6},{6,2},{2,0},{1,5},{5,9},... | collective-permute-start | bytes 1572872 | tf_op jit(solution)/shard_map/ppermute | solution.py:906
  560.5 26.1 %collective-permute-start.57 = (bf16[64,4096]{1,0:T(8,128)(2,1)S(1)}, bf16[64,4096]{1,0:T(8,128)(2,1)S(1)}, u32[]{:S(2)}, u32[]{:S(2)}) collective-permute-start(bf16[64,4096]{1,0:T(8,128)(2,1)S(1)} %get-tuple-element.252), channel_id=1, source_target_pairs={{0,4},{4,8},{8,12},{12,14},{14,10},{10,6},{6,2},{2,0},{1,5},{5,9},... | collective-permute-start | bytes 1572872 | tf_op jit(solution)/shard_map/ppermute | solution.py:906
  560.6 26.0 %collective-permute-start.58 = (bf16[64,4096]{1,0:T(8,128)(2,1)S(1)}, bf16[64,4096]{1,0:T(8,128)(2,1)S(1)}, u32[]{:S(2)}, u32[]{:S(2)}) collective-permute-start(bf16[64,4096]{1,0:T(8,128)(2,1)S(1)} %get-tuple-element.253.refs_3_), channel_id=1, source_target_pairs={{0,2},{4,0},{8,4},{12,8},{14,12},{10,14},{6,10},{2,6},{1,3},{5,1},... | collective-permute-start | bytes 1572872 | tf_op jit(solution)/shard_map/ppermute | solution.py:906
  564.7 26.0 %collective-permute-start.67 = (bf16[64,4096]{1,0:T(8,128)(2,1)S(1)}, bf16[64,4096]{1,0:T(8,128)(2,1)S(1)}, u32[]{:S(2)}, u32[]{:S(2)}) collective-permute-start(bf16[64,4096]{1,0:T(8,128)(2,1)S(1)} %get-tuple-element.271), channel_id=1, source_target_pairs={{0,4},{4,8},{8,12},{12,14},{14,10},{10,6},{6,2},{2,0},{1,5},{5,9},... | collective-permute-start | bytes 1572872 | tf_op jit(solution)/shard_map/ppermute | solution.py:906
  564.9 25.9 %collective-permute-start.68 = (bf16[64,4096]{1,0:T(8,128)(2,1)S(1)}, bf16[64,4096]{1,0:T(8,128)(2,1)S(1)}, u32[]{:S(2)}, u32[]{:S(2)}) collective-permute-start(bf16[64,4096]{1,0:T(8,128)(2,1)S(1)} %get-tuple-element.258.refs_4_.refs_2_), channel_id=1, source_target_pairs={{0,2},{4,0},{8,4},{12,8},{14,12},{10,14},{6,10},{2,6},{1,3},{5,1},... | collective-permute-start | bytes 1572872 | tf_op jit(solution)/shard_map/ppermute | solution.py:906
  (176 other events, 1565.8 us)

commit v2 on v1

--- a/solution.py
+++ b/solution.py
@@ -382,8 +382,8 @@
     return jnp.where(lane // (LANES // 2) == head, vals, jnp.zeros_like(vals))
 
 
-def scores_of(keys, queries, scale, diagonal):
-    scores = dot_nt(keys, queries) * scale
+def scores_of(keys, queries, diagonal):
+    scores = dot_nt(keys, queries)
     if diagonal:
         key_at = lax.broadcasted_iota(jnp.int32, scores.shape, 0)
         query_at = lax.broadcasted_iota(jnp.int32, scores.shape, 1)
@@ -407,9 +407,9 @@
         queries = q_s[rows]
         outs = []
         for head in range(2):
-            picked = head_of(queries, head)
+            picked = head_of(queries, head) * scale
             parts = [
-                scores_of(k_s[i * tile : (i + 1) * tile], picked, scale, i == t)
+                scores_of(k_s[i * tile : (i + 1) * tile], picked, i == t)
                 for i in range(t + 1)
             ]
             top = functools.reduce(
@@ -423,10 +423,10 @@
             for i, p in enumerate(parts):
                 term = dot_nn(
                     vt_s[head * head_size : (head + 1) * head_size, i * tile : (i + 1) * tile],
-                    (p * inverse).astype(bf16),
+                    p.astype(bf16),
                 )
                 acc = term if acc is None else acc + term
-            outs.append(acc)
+            outs.append(acc * inverse)
         o_s[rows] = jnp.concatenate(outs, axis=0).T.astype(bf16)
     sort_out(loc_ref, o_s, o_ref, half_rows)
 
@@ -472,13 +472,13 @@
         rows = slice(t * tile, (t + 1) * tile)
         outs = []
         for head in range(2):
-            queries = head_of(q_s[rows], head)
+            queries = head_of(q_s[rows], head) * scale
             grads = head_of(da_s[rows], head)
             lse = lse_ref[head : head + 1, rows]
             probs, dprobs, row_dot = [], [], 0.0
             for i in range(t + 1):
                 keys = slice(i * tile, (i + 1) * tile)
-                p = jnp.exp(scores_of(k_s[keys], queries, scale, i == t) - lse)
+                p = jnp.exp(scores_of(k_s[keys], queries, i == t) - lse)
                 dp = dot_nt(v_s[keys], grads)
                 row_dot = row_dot + jnp.sum(p * dp, axis=0, keepdims=True)
                 dv_s[keys] += dot_nn(p.astype(bf16), grads)
@@ -487,11 +487,11 @@
             acc = None
             for i in range(t + 1):
                 keys = slice(i * tile, (i + 1) * tile)
-                ds = (probs[i] * (dprobs[i] - row_dot) * scale).astype(bf16)
+                ds = (probs[i] * (dprobs[i] - row_dot)).astype(bf16)
                 dk_s[keys] += dot_nn(ds, queries)
                 term = dot_nn(kt_s[head * head_size : (head + 1) * head_size, keys], ds)
                 acc = term if acc is None else acc + term
-            outs.append(acc)
+            outs.append(acc * scale)
         dq_s[rows] = jnp.concatenate(outs, axis=0).T.astype(bf16)
     sort_out(loc_ref, dq_s, out_ref, half_rows, 0)
     k_s[...] = dk_s[...].astype(bf16)

time: 618 us -> 616 us (level)
  no operation moved by 1% of the time
where the time goes in v2:
time: 616 us; the launch traced here: 605 us
  Pallas kernels  214 us (35%)
  waiting for transfers between devices  188 us (31%)
  starting transfers between devices  127 us (21%)
  local copies, waits for them, and re-layouts  69.5 us (11%)
    pallas_call x42, Pallas kernels, local_call(): pl.pallas_call(functools.partial(local_kernel, body, near_in, near_out, l...  184 us
    ppermute x48, waiting for transfers between devices, ring_shift(): return lax.ppermute(vals, axis, pairs)  99.5 us
    unnamed x239, local copies, waits for them, and re-layouts  64.3 us
    all_to_all x11, starting transfers between devices, exchange(): return lax.all_to_all(vals, 'ctx', split_axis=0, concat_axis=0, tiled=True)  56.7 us
    ppermute x48, starting transfers between devices, ring_shift(): return lax.ppermute(vals, axis, pairs)  55.6 us
    ppermute x3, waiting for transfers between devices, butterfly_sum(): got = lax.ppermute(vals, axis, [(i, i ^ by) for i in range(count)])  37 us
    pallas_call x15, Pallas kernels, put(): pl.pallas_call(functools.partial(ring_put_kernel, starts, tuple((k % coun...  30.1 us
    all_to_all x11, waiting for transfers between devices, exchange(): return lax.all_to_all(vals, 'ctx', split_axis=0, concat_axis=0, tiled=True)  22.3 us
  transfers between devices with their start and end apart: 84, of which 40 were waited for; matrix products, arithmetic and copies ran while one was open for 2% of the time, Pallas kernels for 32%

profile of v2, /device:TPU:0, one launch (start us, length us, event | category | flops | bytes accessed | tf_op | source)
XLA Modules:
  0.0 605.5 jit_solution(6730058311235886136)
XLA Ops:
  15.4 7.2 %all-to-all-start = ((bf16[8,3,128,128]{3,2,1,0:T(8,128)(2,1)}), bf16[8,3,128,128]{3,2,1,0:T(8,128)(2,1)}, u32[]{:S(2)}, u32[]{:S(2)}) async-start(bf16[8,3,128,128]{3,2,1,0:T(8,128)(2,1)} %get-tuple-element.148), calls=%async_computation | async-start | bytes 1572864 | tf_op jit(solution)/shard_map/all_to_all | solution.py:1206
  24.8 7.6 %mlp_forward.3.refs_2_.refs_4_ = f32[128,1024]{1,0:T(8,128)S(1)} custom-call(s32[2]{0:T(128)S(1)} %pad_add_fusion.refs_0_, bf16[2,128,512]{2,1,0:T(8,128)(2,1)S(1)} %copy-done.87, bf16[2,128,512]{2,1,0:T(8,128)(2,1)S(1)} %copy-done.89, f32[1,4096]{1,0:T(1,128)S(1)} %bitcast.60, f32[1,1024]{1,0:T(1,128)S(1)} %get-tuple-element.320.refs_4_, ...), custom_call_target="tpu_custom_call" | custom-call | flops 1 | bytes 1 | tf_op jit(solution)/shard_map/mlp_forward/pallas_call | solution.py:210
  33.3 9.9 %all-to-all-done.refs_1_ = bf16[8,3,128,128]{3,2,1,0:T(8,128)(2,1)} async-done(((bf16[8,3,128,128]{3,2,1,0:T(8,128)(2,1)}), bf16[8,3,128,128]{3,2,1,0:T(8,128)(2,1)}, u32[]{:S(2)}, u32[]{:S(2)}) %all-to-all-start) | async-done | bytes 786464 | tf_op jit(solution)/shard_map/all_to_all | solution.py:1206
  94.7 8.5 %mlp_forward.4 = (f32[128,1024]{1,0:T(8,128)S(1)}, bf16[4096,128]{1,0:T(8,128)(2,1)S(1)}, bf16[2048,128]{1,0:T(8,128)(2,1)S(1)}, bf16[2048,128]{1,0:T(8,128)(2,1)}) custom-call(s32[2]{0:T(128)S(1)} %pad_add_fusion.refs_0_, bf16[2,128,512]{2,1,0:T(8,128)(2,1)S(1)} %copy-done.16, bf16[2,128,512]{2,1,0:T(8,128)(2,1)S(1)} %copy-done.91, f32[1,4096]{1,0:T(1,128)S(1)} %bitcast.61, ...), custom_call_target="tpu_custom_call" | custom-call | flops 1 | bytes 1 | tf_op jit(solution)/shard_map/mlp_forward/pallas_call | solution.py:210
  105.3 10.3 %mlp_backward.3 = (bf16[4096,128]{1,0:T(8,128)(2,1)}, f32[128,1024]{1,0:T(8,128)S(1)}) custom-call(s32[2]{0:T(128)S(1)} %pad_add_fusion.refs_0_, bf16[128,1024]{1,0:T(8,128)(2,1)S(1)} %copy-done.43, bf16[4096,128]{1,0:T(8,128)(2,1)S(1)} %get-tuple-element.164.refs_2_, bf16[512,4096]{1,0:T(8,128)(2,1)} %bitcast.69, ...), custom_call_target="tpu_custom_call" | custom-call | flops 1 | bytes 1 | tf_op jit(solution)/shard_map/mlp_backward/pallas_call | solution.py:210
  123.7 6.2 %all-to-all-start.5 = ((bf16[8,128,128]{2,1,0:T(8,128)(2,1)}), bf16[8,128,128]{2,1,0:T(8,128)(2,1)}, u32[]{:S(2)}, u32[]{:S(2)}) async-start(bf16[8,128,128]{2,1,0:T(8,128)(2,1)} %get-tuple-element.168), calls=%async_computation.5 | async-start | bytes 524288 | tf_op jit(solution)/shard_map/all_to_all | solution.py:1206
  130.0 7.5 %attention_backward.3.refs_7_ = bf16[8,3,128,128]{3,2,1,0:T(8,128)(2,1)} custom-call(s32[16]{0:T(128)S(1)} %add_reduce_fusion.refs_0_, bf16[8,128,128]{2,1,0:T(8,128)(2,1)} %all-to-all-done.2.refs_1_, bf16[8,3,128,128]{3,2,1,0:T(8,128)(2,1)S(1)} %all-to-all-done.3.refs_1_.refs_2_, f32[2,1024]{1,0:T(2,128)S(1)} %get-tuple-element.166.refs_3_, ...), custom_call_target="tpu_custom_call" | custom-call | flops 1 | bytes 1 | tf_op jit(solution)/shard_map/attention_backward/pallas_call | solution.py:210
  176.7 6.5 %section_input_grad.3 = (bf16[8,3,128,128]{3,2,1,0:T(8,128)(2,1)}, bf16[128,1024]{1,0:T(8,128)(2,1)S(1)}, f32[4,1024]{1,0:T(4,128)}) custom-call(s32[2]{0:T(128)S(1)} %pad_add_fusion.refs_0_, bf16[8,3,128,128]{3,2,1,0:T(8,128)(2,1)} %all-to-all-done.4.refs_1_, f32[3,128,128]{2,1,0:T(8,128)S(1)} %pad_maximum_fusion.refs_4_.refs_2_, ...), custom_call_target="tpu_custom_call" | custom-call | flops 1 | bytes 1 | tf_op jit(solution)/shard_map/section_input_grad/pallas_call | solution.py:210
  184.8 8.5 %mlp_forward.5 = (f32[128,1024]{1,0:T(8,128)S(1)}, bf16[4096,128]{1,0:T(8,128)(2,1)S(1)}, bf16[2048,128]{1,0:T(8,128)(2,1)S(1)}, bf16[2048,128]{1,0:T(8,128)(2,1)}) custom-call(s32[2]{0:T(128)S(1)} %pad_add_fusion.refs_0_, bf16[2,128,512]{2,1,0:T(8,128)(2,1)S(1)} %copy-done.20, bf16[2,128,512]{2,1,0:T(8,128)(2,1)S(1)} %copy-done.85, f32[1,4096]{1,0:T(1,128)S(1)} %bitcast.62, ...), custom_call_target="tpu_custom_call" | custom-call | flops 1 | bytes 1 | tf_op jit(solution)/shard_map/mlp_forward/pallas_call | solution.py:210
  198.5 5.9 all-to-all-start.7
  214.9 6.8 %attention_backward.4.refs_7_ = bf16[8,3,128,128]{3,2,1,0:T(8,128)(2,1)S(1)} custom-call(s32[16]{0:T(128)S(1)} %add_reduce_fusion.refs_0_, bf16[8,128,128]{2,1,0:T(8,128)(2,1)} %all-to-all-done.7.refs_1_, bf16[8,3,128,128]{3,2,1,0:T(8,128)(2,1)} %all-to-all-done.6.refs_1_.refs_2_, f32[2,1024]{1,0:T(2,128)S(1)} %get-tuple-element.184.refs_3_, ...), custom_call_target="tpu_custom_call" | custom-call | flops 1 | bytes 1 | tf_op jit(solution)/shard_map/attention_backward/pallas_call | solution.py:210
  229.6 10.0 %mlp_backward.4 = (bf16[4096,128]{1,0:T(8,128)(2,1)S(1)}, f32[128,1024]{1,0:T(8,128)S(1)}) custom-call(s32[2]{0:T(128)S(1)} %pad_add_fusion.refs_0_, bf16[128,1024]{1,0:T(8,128)(2,1)S(1)} %get-tuple-element.183.refs_2_.refs_1_.refs_5_.refs_6_.refs_14_, bf16[4096,128]{1,0:T(8,128)(2,1)S(1)} %copy-done.64, bf16[512,4096]{1,0:T(8,128)(2,1)} %bitcast.71, ...), custom_call_target="tpu_custom_call" | custom-call | flops 1 | bytes 1 | tf_op jit(solution)/shard_map/mlp_backward/pallas_call | solution.py:210
  256.3 9.7 %collective-permute-done.16.refs_2_ = bf16[128,1024]{1,0:T(8,128)(2,1)S(1)} collective-permute-done((bf16[128,1024]{1,0:T(8,128)(2,1)S(1)}, bf16[128,1024]{1,0:T(8,128)(2,1)S(1)}, u32[]{:S(2)}, u32[]{:S(2)}) %collective-permute-start.16) | collective-permute-done | bytes 262176 | tf_op jit(solution)/shard_map/ppermute | solution.py:1103
  287.2 6.4 %collective-permute-done.18.refs_1_ = bf16[256,512]{1,0:T(8,128)(2,1)S(1)} collective-permute-done((bf16[256,512]{1,0:T(8,128)(2,1)S(1)}, bf16[256,512]{1,0:T(8,128)(2,1)S(1)}, u32[]{:S(2)}, u32[]{:S(2)}) %collective-permute-start.18) | collective-permute-done | bytes 262176 | tf_op jit(solution)/shard_map/ppermute | solution.py:906
  300.0 10.3 %mlp_backward.5 = (bf16[4096,128]{1,0:T(8,128)(2,1)}, f32[128,1024]{1,0:T(8,128)S(1)}) custom-call(s32[2]{0:T(128)S(1)} %pad_add_fusion.refs_0_, bf16[128,1024]{1,0:T(8,128)(2,1)S(1)} %copy-done.11, bf16[4096,128]{1,0:T(8,128)(2,1)S(1)} %copy-done.14, bf16[512,4096]{1,0:T(8,128)(2,1)} %bitcast.72, bf16[512,4096]{1,0:T(8,128)(2,1)} %collective-permute-done.2.refs_6_.refs_4_, ...), custom_call_target="tpu_custom_call" | custom-call | flops 1 | bytes 1 | tf_op jit(solution)/shard_map/mlp_backward/pallas_call | solution.py:210
  312.2 6.6 %attention_backward.5.refs_4_ = bf16[8,3,128,128]{3,2,1,0:T(8,128)(2,1)S(1)} custom-call(s32[16]{0:T(128)S(1)} %add_reduce_fusion.refs_0_, bf16[8,2,128,128]{3,2,1,0:T(8,128)(2,1)} %all-to-all-done.9.refs_1_, bf16[8,3,128,128]{3,2,1,0:T(8,128)(2,1)S(1)} %all-to-all-done.3.refs_1_.refs_2_, f32[2,1024]{1,0:T(2,128)S(1)} %get-tuple-element.166.refs_3_, ...), custom_call_target="tpu_custom_call" | custom-call | flops 1 | bytes 1 | tf_op jit(solution)/shard_map/attention_backward/pallas_call | solution.py:210
  334.2 7.4 %up_grad.1 = (bf16[512,4096]{1,0:T(8,128)(2,1)}, bf16[64,2048]{1,0:T(8,128)(2,1)S(1)}, bf16[64,2048]{1,0:T(8,128)(2,1)S(1)}, f32[1,4096]{1,0:T(1,128)S(1)}) custom-call(s32[8]{0:T(128)S(1)} %and_select_fusion.refs_0_.idx_ref, bf16[2,128,512]{2,1,0:T(8,128)(2,1)S(1)} %copy-done.17, bf16[2,128,512]{2,1,0:T(8,128)(2,1)S(1)} %copy-done.21, ...), custom_call_target="tpu_custom_call" | custom-call | flops 1 | bytes 1 | tf_op jit(solution)/shard_map/up_grad/pallas_call | solution.py:210
  341.6 8.1 %collective-permute-done.22.refs_1_ = bf16[256,1024]{1,0:T(8,128)(2,1)S(1)} collective-permute-done((bf16[256,1024]{1,0:T(8,128)(2,1)S(1)}, bf16[256,1024]{1,0:T(8,128)(2,1)S(1)}, u32[]{:S(2)}, u32[]{:S(2)}) %collective-permute-start.22) | collective-permute-done | bytes 524320 | tf_op jit(solution)/shard_map/ppermute | solution.py:906
  361.8 14.6 %collective-permute-done.27.refs_1_ = bf16[64,2048]{1,0:T(8,128)(2,1)S(1)} collective-permute-done((bf16[64,2048]{1,0:T(8,128)(2,1)S(1)}, bf16[64,2048]{1,0:T(8,128)(2,1)S(1)}, u32[]{:S(2)}, u32[]{:S(2)}) %collective-permute-start.27) | collective-permute-done | bytes 262176 | tf_op jit(solution)/shard_map/ppermute | solution.py:906
  413.3 7.2 %attn_grad.1 = (bf16[512,4096]{1,0:T(8,128)(2,1)}, bf16[64,2048]{1,0:T(8,128)(2,1)S(1)}, bf16[64,2048]{1,0:T(8,128)(2,1)S(1)}, f32[1,4096]{1,0:T(1,128)S(1)}) custom-call(s32[8]{0:T(128)S(1)} %and_select_fusion.refs_0_.idx_ref, bf16[2,128,512]{2,1,0:T(8,128)(2,1)S(1)} %copy-done.18, bf16[2,128,512]{2,1,0:T(8,128)(2,1)S(1)} %copy-done.22, ...), custom_call_target="tpu_custom_call" | custom-call | flops 1 | bytes 1 | tf_op jit(solution)/shard_map/attn_grad/pallas_call | solution.py:210
  445.1 7.1 %collective-permute-done.39.refs_1_ = bf16[64,4096]{1,0:T(8,128)(2,1)S(1)} collective-permute-done((bf16[64,4096]{1,0:T(8,128)(2,1)S(1)}, bf16[64,4096]{1,0:T(8,128)(2,1)S(1)}, u32[]{:S(2)}, u32[]{:S(2)}) %collective-permute-start.39) | collective-permute-done | bytes 524320 | tf_op jit(solution)/shard_map/ppermute | solution.py:906
  490.6 6.6 %collective-permute-done.47.refs_1_ = bf16[64,4096]{1,0:T(8,128)(2,1)S(1)} collective-permute-done((bf16[64,4096]{1,0:T(8,128)(2,1)S(1)}, bf16[64,4096]{1,0:T(8,128)(2,1)S(1)}, u32[]{:S(2)}, u32[]{:S(2)}) %collective-permute-start.47) | collective-permute-done | bytes 524320 | tf_op jit(solution)/shard_map/ppermute | solution.py:906
  530.5 20.8 %collective-permute-done.64.refs_1_ = f32[12,512]{1,0:T(8,128)S(1)} collective-permute-done((f32[12,512]{1,0:T(8,128)S(1)}, f32[12,512]{1,0:T(8,128)S(1)}, u32[]{:S(2)}, u32[]{:S(2)}) %collective-permute-start.64) | collective-permute-done | bytes 24608 | tf_op jit(solution)/shard_map/ppermute | solution.py:1088
  569.0 16.2 %collective-permute-done.66.refs_1_ = f32[12,512]{1,0:T(8,128)S(1)} collective-permute-done((f32[12,512]{1,0:T(8,128)S(1)}, f32[12,512]{1,0:T(8,128)S(1)}, u32[]{:S(2)}, u32[]{:S(2)}) %collective-permute-start.66) | collective-permute-done | bytes 24608 | tf_op jit(solution)/shard_map/ppermute | solution.py:1088
  (486 shorter events, 386.9 us)
Async XLA Ops:
  15.4 27.8 %all-to-all-start = ((bf16[8,3,128,128]{3,2,1,0:T(8,128)(2,1)}), bf16[8,3,128,128]{3,2,1,0:T(8,128)(2,1)}, u32[]{:S(2)}, u32[]{:S(2)}) async-start(bf16[8,3,128,128]{3,2,1,0:T(8,128)(2,1)} %get-tuple-element.148), calls=%async_computation | async-start | bytes 1572864 | tf_op jit(solution)/shard_map/all_to_all | solution.py:1206
  22.6 32.6 %collective-permute-start.4 = (bf16[512,1024]{1,0:T(8,128)(2,1)S(1)}, bf16[512,1024]{1,0:T(8,128)(2,1)S(1)}, u32[]{:S(2)}, u32[]{:S(2)}) collective-permute-start(bf16[512,1024]{1,0:T(8,128)(2,1)S(1)} %bitcast.53), channel_id=1, source_target_pairs={{0,1},{1,0},{2,3},{3,2},{4,5},{5,4},{6,7},{7,6},{8,9},{9,8},{10,11... | collective-permute-start | bytes 3145736 | tf_op jit(solution)/shard_map/ppermute | solution.py:1098
  87.1 30.0 %all-to-all-start.3 = ((bf16[8,3,128,128]{3,2,1,0:T(8,128)(2,1)}), bf16[8,3,128,128]{3,2,1,0:T(8,128)(2,1)S(1)}, u32[]{:S(2)}, u32[]{:S(2)}) async-start(bf16[8,3,128,128]{3,2,1,0:T(8,128)(2,1)} %get-tuple-element.161), calls=%async_computation.3 | async-start | bytes 1572864 | tf_op jit(solution)/shard_map/all_to_all | solution.py:1206
  104.8 25.2 %collective-permute-start.7 = (bf16[2048,128]{1,0:T(8,128)(2,1)}, bf16[2048,128]{1,0:T(8,128)(2,1)}, u32[]{:S(2)}, u32[]{:S(2)}) collective-permute-start(bf16[2048,128]{1,0:T(8,128)(2,1)} %get-tuple-element.167), channel_id=1, source_target_pairs={{0,1},{1,0},{2,3},{3,2},{4,5},{5,4},{6,7},{7,6},{8,9},{9,8},{10,11... | collective-permute-start | bytes 1572872 | tf_op jit(solution)/shard_map/ppermute | solution.py:1098
  139.1 26.9 %all-to-all-start.4 = ((bf16[8,3,128,128]{3,2,1,0:T(8,128)(2,1)}), bf16[8,3,128,128]{3,2,1,0:T(8,128)(2,1)}, u32[]{:S(2)}, u32[]{:S(2)}) async-start(bf16[8,3,128,128]{3,2,1,0:T(8,128)(2,1)} %attention_backward.3.refs_7_), calls=%async_computation.4 | async-start | bytes 1572864 | tf_op jit(solution)/shard_map/all_to_all | solution.py:1206
  166.1 32.4 %all-to-all-start.6 = ((bf16[8,3,128,128]{3,2,1,0:T(8,128)(2,1)}), bf16[8,3,128,128]{3,2,1,0:T(8,128)(2,1)}, u32[]{:S(2)}, u32[]{:S(2)}) async-start(bf16[8,3,128,128]{3,2,1,0:T(8,128)(2,1)} %get-tuple-element.173), calls=%async_computation.6 | async-start | bytes 1572864 | tf_op jit(solution)/shard_map/all_to_all | solution.py:1206
  222.6 24.4 %all-to-all-start.8 = ((bf16[8,3,128,128]{3,2,1,0:T(8,128)(2,1)}), bf16[8,3,128,128]{3,2,1,0:T(8,128)(2,1)}, u32[]{:S(2)}, u32[]{:S(2)}) async-start(bf16[8,3,128,128]{3,2,1,0:T(8,128)(2,1)} %copy-done.3), calls=%async_computation.8 | async-start | bytes 1572864 | tf_op jit(solution)/shard_map/all_to_all | solution.py:1206
  269.3 41.8 %all-to-all-start.9 = ((bf16[8,2,128,128]{3,2,1,0:T(8,128)(2,1)}), bf16[8,2,128,128]{3,2,1,0:T(8,128)(2,1)}, u32[]{:S(2)}, u32[]{:S(2)}) async-start(bf16[8,2,128,128]{3,2,1,0:T(8,128)(2,1)} %copy-done.77), calls=%async_computation.9 | async-start | bytes 1048576 | tf_op jit(solution)/shard_map/all_to_all | solution.py:1206
  297.8 26.4 %collective-permute-start.20 = (bf16[256,1024]{1,0:T(8,128)(2,1)}, bf16[256,1024]{1,0:T(8,128)(2,1)}, u32[]{:S(2)}, u32[]{:S(2)}) collective-permute-start(bf16[256,1024]{1,0:T(8,128)(2,1)} %get-tuple-element.201), channel_id=1, source_target_pairs={{0,4},{4,8},{8,12},{12,14},{14,10},{10,6},{6,2},{2,0},{1,5},{5,9},... | collective-permute-start | bytes 1572872 | tf_op jit(solution)/shard_map/ppermute | solution.py:906
  299.3 24.9 %collective-permute-start.21 = (bf16[256,1024]{1,0:T(8,128)(2,1)}, bf16[256,1024]{1,0:T(8,128)(2,1)}, u32[]{:S(2)}, u32[]{:S(2)}) collective-permute-start(bf16[256,1024]{1,0:T(8,128)(2,1)} %get-tuple-element.202.refs_7_), channel_id=1, source_target_pairs={{0,2},{4,0},{8,4},{12,8},{14,12},{10,14},{6,10},{2,6},{1,3},{5,1},... | collective-permute-start | bytes 1572872 | tf_op jit(solution)/shard_map/ppermute | solution.py:906
  319.7 63.7 %all-to-all-start.10 = ((bf16[8,3,128,128]{3,2,1,0:T(8,128)(2,1)}), bf16[8,3,128,128]{3,2,1,0:T(8,128)(2,1)}, u32[]{:S(2)}, u32[]{:S(2)}) async-start(bf16[8,3,128,128]{3,2,1,0:T(8,128)(2,1)} %copy-done.5), calls=%async_computation.10 | async-start | bytes 1572864 | tf_op jit(solution)/shard_map/all_to_all | solution.py:1206
  354.0 38.4 %collective-permute-start.25 = (bf16[256,1024]{1,0:T(8,128)(2,1)}, bf16[256,1024]{1,0:T(8,128)(2,1)}, u32[]{:S(2)}, u32[]{:S(2)}) collective-permute-start(bf16[256,1024]{1,0:T(8,128)(2,1)} %get-tuple-element.208), channel_id=1, source_target_pairs={{0,4},{4,8},{8,12},{12,14},{14,10},{10,6},{6,2},{2,0},{1,5},{5,9},... | collective-permute-start | bytes 1572872 | tf_op jit(solution)/shard_map/ppermute | solution.py:906
  359.7 32.6 %collective-permute-start.26 = (bf16[256,1024]{1,0:T(8,128)(2,1)}, bf16[256,1024]{1,0:T(8,128)(2,1)}, u32[]{:S(2)}, u32[]{:S(2)}) collective-permute-start(bf16[256,1024]{1,0:T(8,128)(2,1)} %get-tuple-element.209.refs_4_), channel_id=1, source_target_pairs={{0,2},{4,0},{8,4},{12,8},{14,12},{10,14},{6,10},{2,6},{1,3},{5,1},... | collective-permute-start | bytes 1572872 | tf_op jit(solution)/shard_map/ppermute | solution.py:906
  435.5 29.7 %collective-permute-start.46 = (bf16[64,4096]{1,0:T(8,128)(2,1)S(1)}, bf16[64,4096]{1,0:T(8,128)(2,1)S(1)}, u32[]{:S(2)}, u32[]{:S(2)}) collective-permute-start(bf16[64,4096]{1,0:T(8,128)(2,1)S(1)} %get-tuple-element.228.refs_4_), channel_id=1, source_target_pairs={{0,2},{4,0},{8,4},{12,8},{14,12},{10,14},{6,10},{2,6},{1,3},{5,1},... | collective-permute-start | bytes 1572872 | tf_op jit(solution)/shard_map/ppermute | solution.py:906
  458.0 29.7 %collective-permute-start.50 = (bf16[256,1024]{1,0:T(8,128)(2,1)S(1)}, bf16[256,1024]{1,0:T(8,128)(2,1)S(1)}, u32[]{:S(2)}, u32[]{:S(2)}) collective-permute-start(bf16[256,1024]{1,0:T(8,128)(2,1)S(1)} %get-tuple-element.233.refs_4_), channel_id=1, source_target_pairs={{0,2},{4,0},{8,4},{12,8},{14,12},{10,14},{6,10},{2,6},{1,3},{5,1},... | collective-permute-start | bytes 1572872 | tf_op jit(solution)/shard_map/ppermute | solution.py:906
  480.5 29.7 %collective-permute-start.54 = (bf16[64,4096]{1,0:T(8,128)(2,1)S(1)}, bf16[64,4096]{1,0:T(8,128)(2,1)S(1)}, u32[]{:S(2)}, u32[]{:S(2)}) collective-permute-start(bf16[64,4096]{1,0:T(8,128)(2,1)S(1)} %ring_own.4.refs_0_), channel_id=1, source_target_pairs={{0,2},{4,0},{8,4},{12,8},{14,12},{10,14},{6,10},{2,6},{1,3},{5,1},... | collective-permute-start | bytes 1572872 | tf_op jit(solution)/shard_map/ppermute | solution.py:906
  485.9 25.1 %collective-permute-start.53 = (bf16[64,4096]{1,0:T(8,128)(2,1)S(1)}, bf16[64,4096]{1,0:T(8,128)(2,1)}, u32[]{:S(2)}, u32[]{:S(2)}) collective-permute-start(bf16[64,4096]{1,0:T(8,128)(2,1)S(1)} %ring_own.4.refs_0_), channel_id=1, source_target_pairs={{0,4},{4,8},{8,12},{12,14},{14,10},{10,6},{6,2},{2,0},{1,5},{5,9},... | collective-permute-start | bytes 1572872 | tf_op jit(solution)/shard_map/ppermute | solution.py:906
  524.5 26.9 %collective-permute-start.55 = (bf16[64,4096]{1,0:T(8,128)(2,1)S(1)}, bf16[64,4096]{1,0:T(8,128)(2,1)S(1)}, u32[]{:S(2)}, u32[]{:S(2)}) collective-permute-start(bf16[64,4096]{1,0:T(8,128)(2,1)S(1)} %get-tuple-element.248), channel_id=1, source_target_pairs={{0,4},{4,8},{8,12},{12,14},{14,10},{10,6},{6,2},{2,0},{1,5},{5,9},... | collective-permute-start | bytes 1572872 | tf_op jit(solution)/shard_map/ppermute | solution.py:906
  526.1 33.2 %collective-permute-start.60 = (bf16[64,4096]{1,0:T(8,128)(2,1)S(1)}, bf16[64,4096]{1,0:T(8,128)(2,1)S(1)}, u32[]{:S(2)}, u32[]{:S(2)}) collective-permute-start(bf16[64,4096]{1,0:T(8,128)(2,1)S(1)} %get-tuple-element.247.refs_4_.refs_2_), channel_id=1, source_target_pairs={{0,2},{4,0},{8,4},{12,8},{14,12},{10,14},{6,10},{2,6},{1,3},{5,1},... | collective-permute-start | bytes 1572872 | tf_op jit(solution)/shard_map/ppermute | solution.py:906
  527.9 31.4 %collective-permute-start.59 = (bf16[64,4096]{1,0:T(8,128)(2,1)}, bf16[64,4096]{1,0:T(8,128)(2,1)S(1)}, u32[]{:S(2)}, u32[]{:S(2)}) collective-permute-start(bf16[64,4096]{1,0:T(8,128)(2,1)} %copy-done.108), channel_id=1, source_target_pairs={{0,4},{4,8},{8,12},{12,14},{14,10},{10,6},{6,2},{2,0},{1,5},{5,9},... | collective-permute-start | bytes 1572872 | tf_op jit(solution)/shard_map/ppermute | solution.py:906
  559.3 26.1 %collective-permute-start.57 = (bf16[64,4096]{1,0:T(8,128)(2,1)S(1)}, bf16[64,4096]{1,0:T(8,128)(2,1)S(1)}, u32[]{:S(2)}, u32[]{:S(2)}) collective-permute-start(bf16[64,4096]{1,0:T(8,128)(2,1)S(1)} %get-tuple-element.252), channel_id=1, source_target_pairs={{0,4},{4,8},{8,12},{12,14},{14,10},{10,6},{6,2},{2,0},{1,5},{5,9},... | collective-permute-start | bytes 1572872 | tf_op jit(solution)/shard_map/ppermute | solution.py:906
  559.4 26.0 %collective-permute-start.58 = (bf16[64,4096]{1,0:T(8,128)(2,1)S(1)}, bf16[64,4096]{1,0:T(8,128)(2,1)S(1)}, u32[]{:S(2)}, u32[]{:S(2)}) collective-permute-start(bf16[64,4096]{1,0:T(8,128)(2,1)S(1)} %get-tuple-element.253.refs_3_), channel_id=1, source_target_pairs={{0,2},{4,0},{8,4},{12,8},{14,12},{10,14},{6,10},{2,6},{1,3},{5,1},... | collective-permute-start | bytes 1572872 | tf_op jit(solution)/shard_map/ppermute | solution.py:906
  563.5 26.0 %collective-permute-start.67 = (bf16[64,4096]{1,0:T(8,128)(2,1)S(1)}, bf16[64,4096]{1,0:T(8,128)(2,1)S(1)}, u32[]{:S(2)}, u32[]{:S(2)}) collective-permute-start(bf16[64,4096]{1,0:T(8,128)(2,1)S(1)} %get-tuple-element.271), channel_id=1, source_target_pairs={{0,4},{4,8},{8,12},{12,14},{14,10},{10,6},{6,2},{2,0},{1,5},{5,9},... | collective-permute-start | bytes 1572872 | tf_op jit(solution)/shard_map/ppermute | solution.py:906
  563.6 25.9 %collective-permute-start.68 = (bf16[64,4096]{1,0:T(8,128)(2,1)S(1)}, bf16[64,4096]{1,0:T(8,128)(2,1)S(1)}, u32[]{:S(2)}, u32[]{:S(2)}) collective-permute-start(bf16[64,4096]{1,0:T(8,128)(2,1)S(1)} %get-tuple-element.258.refs_4_.refs_2_), channel_id=1, source_target_pairs={{0,2},{4,0},{8,4},{12,8},{14,12},{10,14},{6,10},{2,6},{1,3},{5,1},... | collective-permute-start | bytes 1572872 | tf_op jit(solution)/shard_map/ppermute | solution.py:906
  (176 other events, 1564.8 us)
